TPU v7x, 512 devices: a whole 4x4x16 slice. The times are simulated.
512 devices in a mesh: dp: 64 (over z_hi, x, y), tensor: 8 (over z_lo, core).
Axes of the slice: x: 4, y: 4, z: 16 (z_hi: 4, z_lo: 4; z = z_hi * 4 + z_lo), core: 2. Of those that a mesh axis runs over, the one named last changes fastest.
Arguments:
- hidden_act: bfloat16 [16384, 1152], P('dp', 'tensor'), may hold values from -6 to 6
- out_grad: bfloat16 [16384, 5120], P('dp', 'tensor'), may hold values from -0.375 to 0.375
- error_in: bfloat16 [64, 1152, 5120], P('dp', 'tensor'), may hold values from -6 to 6
- subspace: bfloat16 [5120, 256], P('tensor', 'dp'), may hold values from -0.078125 to 0.078125
- first_moment: float32 [1152, 256], P('tensor', 'dp'), may hold values from -1.8 to 1.8
- second_moment: float32 [1152, 256], P('tensor', 'dp'), may hold values from 0.0001 to 0.01
Outputs:
- weight_step: bfloat16 [1152, 5120], P('tensor')
- error_out: bfloat16 [64, 1152, 5120], P('dp', 'tensor')
- first_new: float32 [1152, 256], P('tensor', 'dp')
- second_new: float32 [1152, 256], P('tensor', 'dp')
All inputs are finite; a program needn't handle non-finite values.
Results may differ from a plain program's by a relative error of at most 0.0095.
Values may be sent and summed in bfloat16 or wider, within the bound.
No kernel may reach another device: no remote copies, remote signals or barrier semaphores. Data moves between devices by JAX's collectives and lax.ppermute only.
A program may use at most 64 MiB of HBM per device.

v0:
```python
import jax
import jax.numpy as jnp
from jax import lax
from jax.sharding import PartitionSpec as P

STEP = 20


BETA_ONE = 0.9
BETA_TWO = 0.999
EPSILON = 1e-08


def local(hidden_act, out_grad, error_in, subspace, first_moment, second_moment):
    partial_basis = lax.all_gather(subspace, "tensor", axis=0, tiled=True)
    basis = lax.all_gather(partial_basis, "dp", axis=1, tiled=True)
    gradient = jnp.einsum(
        "tr,tc->rc",
        hidden_act,
        lax.all_gather(out_grad, "tensor", axis=1, tiled=True),
        preferred_element_type=jnp.float32,
    ).astype(jnp.bfloat16)
    basis_wide = basis.astype(jnp.float32)
    accumulated = gradient.astype(jnp.float32) + error_in[0].astype(jnp.float32)
    projected = jnp.dot(accumulated, basis_wide, precision=lax.Precision.HIGHEST)
    back = lax.dot_general(
        projected, basis_wide, (((1,), (1,)), ((), ())), precision=lax.Precision.HIGHEST
    )
    error_out = (accumulated - back).astype(jnp.bfloat16)[None]
    proj_sum = lax.psum_scatter(projected, "dp", scatter_dimension=1, tiled=True)
    mean_proj = proj_sum / lax.axis_size("dp")
    first_new = BETA_ONE * first_moment + (1.0 - BETA_ONE) * mean_proj
    second_new = BETA_TWO * second_moment + (1.0 - BETA_TWO) * mean_proj * mean_proj
    first_hat = first_new / (1.0 - BETA_ONE**STEP)
    second_hat = second_new / (1.0 - BETA_TWO**STEP)
    update = (first_hat / (jnp.sqrt(second_hat) + EPSILON)).astype(jnp.bfloat16)
    updates_all = lax.all_gather(update, "dp", axis=1, tiled=True)
    weight_step = lax.dot_general(
        updates_all, basis, (((1,), (1,)), ((), ())), preferred_element_type=jnp.float32
    ).astype(jnp.bfloat16)
    return (weight_step, error_out, first_new, second_new)


def solution(mesh):
    placed = (
        P("dp", "tensor"),
        P("dp", "tensor"),
        P("dp", "tensor", None),
        P("tensor", "dp"),
        P("tensor", "dp"),
        P("tensor", "dp"),
    )
    return jax.shard_map(
        local,
        mesh=mesh,
        in_specs=placed,
        out_specs=(
            P("tensor", None),
            P("dp", "tensor", None),
            P("tensor", "dp"),
            P("tensor", "dp"),
        ),
        check_vma=False,
    )
```

profile of v0, /device:TPU:32, one launch (start us, length us, event | category | flops | bytes accessed | tf_op | source)
XLA Modules:
  0.0 1193.6 jit_solution(10990841410386279515)
XLA Ops:
  7.2 0.0 copy-start
  7.2 0.0 all-gather.5.cloned.1.call-start
  7.2 0.7 all-gather.5.cloned.1.call-update
  7.9 0.0 all-gather.7.cloned.1.call-start
  8.0 16.8 %all_gather.13 = bf16[5120,4]{0,1:T(4,128)(2,1)} all-gather(bf16[640,4]{0,1:T(4,128)(2,1)} %param.9), channel_id=1, replica_groups=mesh['dp'=64,'tensor'=8] {'tensor'}, dimensions={0}, use_global_device_ids=true | all-gather | bytes 46080 | tf_op jit(solution)/shard_map/all_gather | solution.py:15
  24.7 0.0 all-gather.7.cloned.1.call-update
  24.7 32.2 %all-gather.5.cloned.1.call-done = bf16[256,5120]{1,0:T(8,128)(2,1)} async-done(((bf16[256,640]{1,0:T(8,128)(2,1)}), bf16[256,5120]{1,0:T(8,128)(2,1)}) %all-gather.5.cloned.1.call-update) | async-done | bytes 2621456 | tf_op jit(solution)/shard_map/all_gather | solution.py:20
  57.0 4.3 fusion.2
  61.3 118.2 %all-gather.7.cloned.1.call-done = bf16[64,4,5120]{2,1,0:T(4,128)(2,1)} async-done(((bf16[1,4,5120]{2,1,0:T(4,128)(2,1)}), bf16[64,4,5120]{2,1,0:T(4,128)(2,1)}) %all-gather.7.cloned.1.call-update) | async-done | bytes 2621456 | tf_op jit(solution)/shard_map/all_gather | solution.py:16
  179.5 4.0 reshape.12
  183.6 4.7 fusion.6
  188.2 0.0 copy-start.1
  188.3 0.0 copy-start.2
  188.3 0.0 copy-start.3
  188.3 4.4 fusion.3
  192.7 0.7 all-reduce.3.cloned.1.call-update
  193.5 1.3 dynamic-slice
  195.4 768.1 %all-reduce.3.cloned.1.call-done = f32[144,256]{1,0:T(8,128)} async-done(((f32[144,256]{1,0:T(8,128)}), f32[144,256]{1,0:T(8,128)}) %all-reduce.3.cloned.1.call-update) | async-done | bytes 147472
  963.4 1.0 constant_dynamic-slice_fusion
  964.4 0.1 copy.30
  964.5 0.6 fusion.5
  965.1 220.2 %all-gather.1 = bf16[64,4,144]{2,1,0:T(4,128)(2,1)S(1)} all-gather(bf16[1,4,144]{2,1,0:T(4,128)(2,1)S(1)} %get-tuple-element.16), channel_id=1, replica_groups=mesh['dp'=64,'tensor'=8] {'dp'}, dimensions={0}, use_global_device_ids=true | all-gather | bytes 74880 | tf_op jit(solution)/shard_map/all_gather | solution.py:37
  1185.3 0.1 reshape.14
  1185.4 1.7 convolution_convert_fusion
  (5 shorter events, 0.0 us)
Async XLA Ops:
  7.2 49.8 %copy-start = (bf16[256,144]{0,1:T(8,128)(2,1)S(1)}, bf16[256,144]{0,1:T(8,128)(2,1)}, u32[]{:S(2)}) copy-start(bf16[256,144]{0,1:T(8,128)(2,1)} %param.6) | copy-start | bytes 221188
  7.2 49.8 %all-gather.5.cloned.1.call-start = ((), (), s32[]{:S(2)}) async-start(), calls=%async_computation | async-start | bytes 2949120 | tf_op jit(solution)/shard_map/all_gather | solution.py:20
  7.9 171.6 %all-gather.7.cloned.1.call-start = ((), (), s32[]{:S(2)}) async-start(), calls=%async_computation.1 | async-start | bytes 2662400 | tf_op jit(solution)/shard_map/all_gather | solution.py:16
  188.2 4.5 copy-start.1
  188.3 776.2 %copy-start.2 = (f32[144,4]{0,1:T(4,128)S(1)}, f32[144,4]{0,1:T(4,128)}, u32[]{:S(2)}) copy-start(f32[144,4]{0,1:T(4,128)} %param.10) | copy-start | bytes 6916
  188.3 776.2 %copy-start.3 = (f32[144,4]{0,1:T(4,128)S(1)}, f32[144,4]{0,1:T(4,128)}, u32[]{:S(2)}) copy-start(f32[144,4]{0,1:T(4,128)} %param.11) | copy-start | bytes 6916
  192.7 770.7 %all-reduce.3.cloned.1.call-start = ((), (), s32[]{:S(2)}) async-start(), calls=%async_computation.2 | async-start | bytes 294912
Sparse Core Ops, SparseCore 0:
  10.1 46.8 all-gather.4
  61.1 118.3 all-gather.6
  197.0 766.3 all-reduce.2
where the time goes:
time: 1190 us
  waiting for transfers between devices  920 us (77%)
  blocking collectives  237 us (20%)
  matrix products  15.1 us (1%)
  between operations  14.5 us (1%)
    unnamed x4, waiting for transfers between devices  769 us
    all_gather x1, blocking collectives, local(): updates_all = lax.all_gather(update, 'dp', axis=1, tiled=True)  220 us
    all_gather x1, waiting for transfers between devices, local(): basis = lax.all_gather(partial_basis, 'dp', axis=1, tiled=True)  118 us
    all_gather x1, waiting for transfers between devices, local(): lax.all_gather(out_grad, 'tensor', axis=1, tiled=True)  32.2 us
  transfers between devices with their start and end apart: 3, of which 3 were waited for; matrix products, arithmetic and copies ran while one was open for 0% of the time, Pallas kernels for 0%

commit v1 on v0

v1 whole, which is shorter than its diff:
```python
import jax
import jax.numpy as jnp
from jax import lax
from jax.experimental import pallas as pl
from jax.experimental.pallas import tpu as pltpu
from jax.sharding import Mesh, PartitionSpec as P

STEP = 20
BETA_ONE = 0.9
BETA_TWO = 0.999
EPSILON = 1e-08

AXES = ("zh", "x", "y", "zl", "c")
SIZES = (4, 4, 4, 4, 2)
DP = ("zh", "x", "y")
TENSOR = ("zl", "c")
ROWS, WIDTH, RANK, TOKENS = 144, 640, 256, 256
COLUMNS = 8 * WIDTH
VMEM = 60 * 1024 * 1024
LONG = 60_000_000_000
SHORT = 1_000_000_000
LONG_MERGE = 3_000_000_000
LONG_UPDATE = 17_000_000_000
LONG_FEEDBACK = 10_000_000_000
LONG_GRADIENTS = 9_200_000_000
f32, bf16 = jnp.float32, jnp.bfloat16


def to_all(block, axes, size):
    return lax.all_to_all(jnp.broadcast_to(block[None], (size, *block.shape)), axes, 0, 0)


def swap_cores(block):
    return lax.ppermute(block, "c", [(0, 1), (1, 0)])


def from_xor(block, bits):
    return lax.ppermute(block, "zl", [(i, i ^ bits) for i in range(4)])


def halves(value):
    high = value.astype(bf16)
    return high, (value - high.astype(f32)).astype(bf16)


def call(kernel, name, out_shape, in_specs, out_specs, scratch, cycles):
    return pl.pallas_call(
        kernel,
        out_shape=out_shape,
        in_specs=in_specs,
        out_specs=out_specs,
        scratch_shapes=scratch,
        compiler_params=pltpu.CompilerParams(vmem_limit_bytes=VMEM),
        cost_estimate=pl.CostEstimate(flops=cycles, bytes_accessed=4_000_000, transcendentals=0),
        name=name,
    )


VM, SM, ANY = pl.BlockSpec(memory_space=pltpu.VMEM), pl.BlockSpec(memory_space=pltpu.SMEM), pl.BlockSpec(memory_space=pl.ANY)
CONTRACT = (((1,), (1,)), ((), ()))
BASIS = (16, 4, 16, WIDTH)


def spread_kernel(along_z, out):
    for zl in range(4):
        block = jnp.concatenate([along_z[zh, zl].astype(f32) for zh in range(4)], axis=0).astype(bf16)
        for peer in range(16):
            out[peer, zl] = block


def spread(along_z):
    return call(
        spread_kernel, "spread", jax.ShapeDtypeStruct(BASIS, bf16), [VM], VM, [], LONG
    )(along_z)


def pick_kernel(place, error, out, held, sems, done):
    copies, outs = [], []
    for z in range(4):
        start = pl.multiple_of((2 * z + 1 - place[1]) * WIDTH, 128)
        copies.append(pltpu.make_async_copy(error.at[:, pl.ds(start, WIDTH)], held.at[z], sems.at[z]))
        copies[z].start()
    for z in range(4):
        copies[z].wait()
        outs.append(pltpu.make_async_copy(held.at[z], out.at[z], done.at[z]))
        outs[z].start()
    for copy in outs:
        copy.wait()


def pick(place, error):
    shape = jax.ShapeDtypeStruct((4, ROWS, WIDTH), bf16)
    scratch = [
        pltpu.VMEM((4, ROWS, WIDTH), bf16),
        pltpu.SemaphoreType.DMA((4,)),
        pltpu.SemaphoreType.DMA((4,)),
    ]
    return call(pick_kernel, "pick", shape, [SM, ANY], ANY, scratch, SHORT)(place, error)


ORDER = (0, 1, 2, 3)


def arrived_kernel(first, second, out):
    out[...] = jnp.zeros_like(out)


def arrived(first, second):
    shape = jax.ShapeDtypeStruct((8, 128), f32)
    return call(arrived_kernel, "arrived", shape, [ANY, ANY], VM, [], LONG_GRADIENTS)(first, second)


def accumulate_kernel(
    place, act, act_other, first, second, third, fourth, ready, error, error_other,
    out, acts, grads, errors, totals, sems, pair_sems, done,
):
    zl, core = place[0], place[1]
    heads = [
        pltpu.make_async_copy(act, acts.at[0], pair_sems.at[0]),
        pltpu.make_async_copy(act_other, acts.at[1], pair_sems.at[1]),
    ]
    for copy in heads:
        copy.start()
    copies = []
    for step, source in enumerate((first, second, third, fourth)):
        z = zl ^ ORDER[step]
        start = pl.multiple_of((2 * z + core) * WIDTH, 128)
        moved = [
            pltpu.make_async_copy(source, grads.at[step], sems.at[step, 0]),
            pltpu.make_async_copy(error.at[:, pl.ds(start, WIDTH)], errors.at[0, step], sems.at[step, 1]),
            pltpu.make_async_copy(error_other.at[z], errors.at[1, step], sems.at[step, 2]),
        ]
        for copy in moved:
            copy.start()
        copies.append(moved)
    for copy in heads:
        copy.wait()
    outs = []
    for step in range(4):
        for copy in copies[step]:
            copy.wait()
        for side in range(2):
            gradient = jnp.dot(acts[side], grads[step], preferred_element_type=f32).astype(bf16)
            high, low = halves(gradient.astype(f32) + errors[side, step].astype(f32))
            totals[step, side] = jnp.concatenate([high, low], axis=0)
            outs.append(pltpu.make_async_copy(totals.at[step, side], out.at[step, side], done.at[step, side]))
            outs[-1].start()
    for copy in outs:
        copy.wait()


def accumulate(place, act, act_other, grads, ready, error, error_other):
    return call(
        accumulate_kernel,
        "accumulate",
        jax.ShapeDtypeStruct((4, 2, 2 * ROWS, WIDTH), bf16),
        [SM] + [ANY] * 9,
        ANY,
        [
            pltpu.VMEM((2, ROWS, TOKENS), bf16),
            pltpu.VMEM((4, TOKENS, WIDTH), bf16),
            pltpu.VMEM((2, 4, ROWS, WIDTH), bf16),
            pltpu.VMEM((4, 2, 2 * ROWS, WIDTH), bf16),
            pltpu.SemaphoreType.DMA((4, 3)),
            pltpu.SemaphoreType.DMA((2,)),
            pltpu.SemaphoreType.DMA((4, 2)),
        ],
        SHORT,
    )(place, act, act_other, *grads, ready, error, error_other)


def project_kernel(place, total, own, turned, sums, totals, basis, sems):
    zl, core = place[0], place[1]
    copies = []
    for step in range(4):
        z = zl ^ ORDER[step]
        moved = [
            pltpu.make_async_copy(total.at[step], totals.at[step], sems.at[step, 0]),
            pltpu.make_async_copy(own.at[:, z], basis.at[step], sems.at[step, 1]),
        ]
        for copy in moved:
            copy.start()
        copies.append(moved)
    values = [jnp.zeros((2 * ROWS, RANK), f32)] * 2
    for step in range(4):
        for copy in copies[step]:
            copy.wait()
        part = basis[step].reshape(RANK, WIDTH)
        for side in range(2):
            values[side] += lax.dot_general(totals[step, side], part, CONTRACT, preferred_element_type=f32)
    for side in range(2):
        projected = values[side][:ROWS] + values[side][ROWS:]
        sums[side] = projected
        padded = jnp.concatenate([projected, jnp.zeros((RANK - ROWS, RANK), f32)], axis=0)
        turned[1 - core if side else core] = padded.T[:, :ROWS].astype(bf16)


def project(place, total, own):
    return call(
        project_kernel,
        "project",
        (jax.ShapeDtypeStruct((2, RANK, ROWS), bf16), jax.ShapeDtypeStruct((2, ROWS, RANK), f32)),
        [SM, ANY, ANY],
        (VM, VM),
        [
            pltpu.VMEM((4, 2, 2 * ROWS, WIDTH), bf16),
            pltpu.VMEM((4, 16, 16, WIDTH), bf16),
            pltpu.SemaphoreType.DMA((4, 2)),
        ],
        SHORT,
    )(place, total, own)


def feedback_kernel(
    place, total, sums, received, own, kept, sent, totals, basis, results, sems, done
):
    zl = place[0]
    copies = []
    for step in range(4):
        z = zl ^ ORDER[step]
        moved = [
            pltpu.make_async_copy(total.at[step], totals.at[step], sems.at[step, 0]),
            pltpu.make_async_copy(own.at[:, z], basis.at[step], sems.at[step, 1]),
        ]
        for copy in moved:
            copy.start()
        copies.append(moved)
    backs = []
    for side in range(2):
        backs.append(jnp.concatenate(halves(sums[side] + received[1 - side]), axis=0))
    outs = []
    for step in range(4):
        for copy in copies[step]:
            copy.wait()
        part = basis[step].reshape(RANK, WIDTH)
        for side, target in ((1, sent), (0, kept)):
            back = jnp.dot(backs[side], part, preferred_element_type=f32)
            value = totals[step, side, :ROWS].astype(f32) + totals[step, side, ROWS:].astype(f32)
            results[side, step] = (value - (back[:ROWS] + back[ROWS:])).astype(bf16)
            outs.append(pltpu.make_async_copy(results.at[side, step], target.at[step], done.at[side, step]))
            outs[-1].start()
    for copy in outs:
        copy.wait()


def feedback(place, total, sums, received, own):
    shape = jax.ShapeDtypeStruct((4, ROWS, WIDTH), bf16)
    return call(
        feedback_kernel,
        "feedback",
        (shape, shape),
        [SM, ANY, VM, VM, ANY],
        (ANY, ANY),
        [
            pltpu.VMEM((4, 2, 2 * ROWS, WIDTH), bf16),
            pltpu.VMEM((4, 16, 16, WIDTH), bf16),
            pltpu.VMEM((2, 4, ROWS, WIDTH), bf16),
            pltpu.SemaphoreType.DMA((4, 2)),
            pltpu.SemaphoreType.DMA((2, 4)),
        ],
        LONG_FEEDBACK,
    )(place, total, sums, received, own)


def merge_kernel(place, kept, received, out, held, sems, done):
    zl, core = place[0], place[1]
    copies, outs = [], []
    for step in range(4):
        z = zl ^ ORDER[step]
        for side, source in enumerate((kept, received)):
            start = pl.multiple_of((2 * z + (1 - core if side else core)) * WIDTH, 128)
            copies.append(pltpu.make_async_copy(source.at[step], held.at[:, pl.ds(start, WIDTH)], sems.at[step, side]))
            copies[-1].start()
    for copy in copies:
        copy.wait()
    for part in range(3):
        rows = pl.ds(part * 48, 48)
        outs.append(pltpu.make_async_copy(held.at[rows], out.at[rows], done.at[part]))
        outs[part].start()
    for copy in outs:
        copy.wait()


def merge(place, kept, received):
    shape = jax.ShapeDtypeStruct((ROWS, COLUMNS), bf16)
    scratch = [
        pltpu.VMEM((ROWS, COLUMNS), bf16),
        pltpu.SemaphoreType.DMA((4, 2)),
        pltpu.SemaphoreType.DMA((3,)),
    ]
    return call(merge_kernel, "merge", shape, [SM, ANY, ANY], ANY, scratch, LONG_MERGE)(place, kept, received)


def weight_kernel(place, updates, own, other, out, held, mine, theirs, results, head, sems, done):
    first = place[1] == 0
    pltpu.make_async_copy(updates, held, head.at[0]).start()
    copies = []
    for z in range(4):
        copies.append(pltpu.make_async_copy(own.at[:, z], mine.at[z], sems.at[z, 0]))
        copies.append(pltpu.make_async_copy(other.at[:, z], theirs.at[z], sems.at[z, 1]))
    for copy in copies:
        copy.start()
    pltpu.make_async_copy(updates, held, head.at[0]).wait()
    value = held[...].reshape(RANK, ROWS).astype(f32)
    padded = jnp.concatenate([value, jnp.zeros((RANK, RANK - ROWS), f32)], axis=1)
    turned = padded.T[:ROWS].astype(bf16)
    outs = []
    for z in range(4):
        copies[2 * z].wait()
        copies[2 * z + 1].wait()
        both = mine[z].reshape(RANK, WIDTH), theirs[z].reshape(RANK, WIDTH)
        for core in range(2):
            part = jnp.where(first, both[core], both[1 - core])
            start = (2 * z + core) * WIDTH
            step = jnp.dot(turned, part, preferred_element_type=f32)
            results[:, start : start + WIDTH] = step.astype(bf16)
        columns = pl.ds(z * 2 * WIDTH, 2 * WIDTH)
        outs.append(pltpu.make_async_copy(results.at[:, columns], out.at[:, columns], done.at[z]))
        outs[z].start()
    for copy in outs:
        copy.wait()


def weight(place, updates, own, other):
    return call(
        weight_kernel,
        "weight_step",
        jax.ShapeDtypeStruct((ROWS, COLUMNS), bf16),
        [SM, ANY, ANY, ANY],
        ANY,
        [
            pltpu.VMEM((16, 16, ROWS), bf16),
            pltpu.VMEM((4, 16, 16, WIDTH), bf16),
            pltpu.VMEM((4, 16, 16, WIDTH), bf16),
            pltpu.VMEM((ROWS, COLUMNS), bf16),
            pltpu.SemaphoreType.DMA((1,)),
            pltpu.SemaphoreType.DMA((4, 2)),
            pltpu.SemaphoreType.DMA((4,)),
        ],
        SHORT,
    )(place, updates, own, other)


def combine_kernel(part, first, second, out):
    total = jnp.sum(part[...].astype(f32), axis=0)
    for peer in range(4):
        out[peer, :16] = total
        out[peer, 16:20] = first[...]
        out[peer, 20:] = second[...]


def combine(part, first, second):
    shape = jax.ShapeDtypeStruct((4, 24, ROWS), f32)
    return call(combine_kernel, "combine", shape, [VM] * 3, VM, [], SHORT)(part, first, second)


def moments(first, second, mean):
    first = BETA_ONE * first + (1.0 - BETA_ONE) * mean
    second = BETA_TWO * second + (1.0 - BETA_TWO) * mean * mean
    return first, second


def update_kernel(place, both, out, first_own, second_own, held):
    mean = (both[0, :16] + both[1, :16] + both[2, :16] + both[3, :16]) / 64
    for peer in range(4):
        held[peer] = mean[4 * peer : 4 * peer + 4]
    first = jnp.concatenate([both[peer, 16:20] for peer in range(4)], axis=0)
    second = jnp.concatenate([both[peer, 20:24] for peer in range(4)], axis=0)
    first, second = moments(first, second, mean)
    first_hat = first / (1.0 - BETA_ONE**STEP)
    second_hat = second / (1.0 - BETA_TWO**STEP)
    update = (first_hat / (jnp.sqrt(second_hat) + EPSILON)).astype(bf16)
    for peer in range(16):
        out[peer] = update
    zh = place[2]
    mine = held[zh]
    first_own[...], second_own[...] = moments(both[zh, 16:20], both[zh, 20:24], mine)


def new_update(place, both):
    shape = jax.ShapeDtypeStruct((4, ROWS), f32)
    return call(
        update_kernel,
        "update",
        (jax.ShapeDtypeStruct((16, 16, ROWS), bf16), shape, shape),
        [SM, VM],
        (VM, VM, VM),
        [pltpu.VMEM((4, 4, ROWS), f32)],
        LONG_UPDATE,
    )(place, both)


def local(hidden_act, out_grad, error_in, subspace, first_moment, second_moment):
    zh = lax.axis_index("zh")
    place = jnp.stack([lax.axis_index("zl"), lax.axis_index("c"), zh]).astype(jnp.int32)
    act = hidden_act.T

    along_z = to_all(subspace.T, ("zh", "zl"), 16)
    spreading = spread(along_z.reshape(4, 4, 4, WIDTH))
    own = lax.all_to_all(spreading, ("x", "y"), 0, 0)
    error = error_in[0]
    grads = [out_grad] + [from_xor(out_grad, bits) for bits in ORDER[1:]]
    error_other = swap_cores(pick(place, error))
    ready = arrived(grads[2], grads[3])
    total = accumulate(place, act, swap_cores(act), grads, ready, error, error_other)
    own, total = lax.optimization_barrier((own, total))
    turned, sums = project(place, total, own)

    part = lax.all_to_all(turned.reshape(32, 16, ROWS), ("c", "x", "y"), 0, 0)
    received = swap_cores(sums)
    error_kept, error_sent = feedback(place, total, sums, received, own)
    part, error_kept, error_sent, later = lax.optimization_barrier((part, error_kept, error_sent, own))
    other = swap_cores(later)
    error_received = swap_cores(error_sent)
    both = combine(part, first_moment.T, second_moment.T)
    both = lax.all_to_all(both, "zh", 0, 0)
    error_received, other = lax.optimization_barrier((error_received, other))
    error_out = merge(place, error_kept, error_received)
    update, first_own, second_own = new_update(place, both)
    updates = lax.all_to_all(update, ("x", "y"), 0, 0)
    weight_step = weight(place, updates, own, other)
    return (weight_step, error_out[None], first_own.T, second_own.T)


def solution(mesh):
    fine = Mesh(mesh.devices.reshape(SIZES), AXES)
    placed = (
        P(DP, TENSOR),
        P(DP, TENSOR),
        P(DP, TENSOR, None),
        P(TENSOR, DP),
        P(TENSOR, DP),
        P(TENSOR, DP),
    )
    return jax.shard_map(
        local,
        mesh=fine,
        in_specs=placed,
        out_specs=(P(TENSOR, None), P(DP, TENSOR, None), P(TENSOR, DP), P(TENSOR, DP)),
        check_vma=False,
    )
```

time: 1190 us -> 129 us (0.11)
  the two profiles are of different devices: /device:TPU:32 before, /device:TPU:2 now
where the time goes in v1:
time: 129 us; the launch traced here: 128 us
  starting transfers between devices  65.3 us (51%)
  Pallas kernels  30.4 us (24%)
  waiting for transfers between devices  22.1 us (17%)
  local copies, waits for them, and re-layouts  8.83 us (7%)
    all_to_all x1, starting transfers between devices, to_all(): lax.all_to_all(jnp.broadcast_to(block[None], (size, *block.shape)), axes,...  15.2 us
    ppermute x3, starting transfers between devices, from_xor(): return lax.ppermute(block, 'zl', [(i, i ^ bits) for i in range(4)])  11 us
    all_to_all x1, waiting for transfers between devices, local(): both = lax.all_to_all(both, 'zh', 0, 0)  10.8 us
    ppermute x5, starting transfers between devices, swap_cores(): return lax.ppermute(block, 'c', [(0, 1), (1, 0)])  10.6 us
    all_to_all x1, starting transfers between devices, local(): both = lax.all_to_all(both, 'zh', 0, 0)  8.69 us
    all_to_all x1, starting transfers between devices, local(): own = lax.all_to_all(spreading, ('x', 'y'), 0, 0)  7.61 us
    unnamed x32, local copies, waits for them, and re-layouts  7.48 us
    all_to_all x1, starting transfers between devices, local(): part = lax.all_to_all(turned.reshape(32, 16, ROWS), ('c', 'x', 'y'), 0, 0)  7.47 us
  transfers between devices with their start and end apart: 13, of which 4 were waited for; matrix products, arithmetic and copies ran while one was open for 1% of the time, Pallas kernels for 15%

profile of v1, /device:TPU:2, one launch (start us, length us, event | category | flops | bytes accessed | tf_op | source)
XLA Modules:
  0.0 128.1 jit_solution(9844761365068693014)
XLA Ops:
  2.0 15.2 %all-to-all-start = ((bf16[16,4,640]{2,1,0:T(4,128)(2,1)}), bf16[16,4,640]{2,1,0:T(4,128)(2,1)S(1)}, u32[]{:S(2)}, u32[]{:S(2)}) async-start(bf16[16,4,640]{2,1,0:T(4,128)(2,1)} %broadcast_in_dim.4), calls=%async_computation | async-start | bytes 163840 | tf_op jit(solution)/shard_map/all_to_all | solution.py:30
  17.2 4.7 %collective-permute-start.2 = (bf16[256,640]{1,0:T(8,128)(2,1)}, bf16[256,640]{1,0:T(8,128)(2,1)S(1)}, u32[]{:S(2)}, u32[]{:S(2)}) collective-permute-start(bf16[256,640]{1,0:T(8,128)(2,1)} %first.1), channel_id=1, source_target_pairs={{0,4},{2,6},{4,0},{6,2},{1,5},{3,7},{5,1},{7,3},{8,12},{10,14},{12... | collective-permute-start | bytes 983048 | tf_op jit(solution)/shard_map/ppermute | solution.py:38
  21.9 3.4 %collective-permute-start.3 = (bf16[256,640]{1,0:T(8,128)(2,1)}, bf16[256,640]{1,0:T(8,128)(2,1)S(1)}, u32[]{:S(2)}, u32[]{:S(2)}) collective-permute-start(bf16[256,640]{1,0:T(8,128)(2,1)} %first.1), channel_id=1, source_target_pairs={{0,6},{2,4},{4,2},{6,0},{1,7},{3,5},{5,3},{7,1},{8,14},{10,12},{12... | collective-permute-start | bytes 983048 | tf_op jit(solution)/shard_map/ppermute | solution.py:38
  25.3 5.3 %all-to-all-done = bf16[16,4,640]{2,1,0:T(4,128)(2,1)S(1)} async-done(((bf16[16,4,640]{2,1,0:T(4,128)(2,1)}), bf16[16,4,640]{2,1,0:T(4,128)(2,1)S(1)}, u32[]{:S(2)}, u32[]{:S(2)}) %all-to-all-start) | async-done | bytes 81952 | tf_op jit(solution)/shard_map/all_to_all | solution.py:30
  31.3 2.1 %spread.1 = bf16[16,4,16,640]{3,2,1,0:T(8,128)(2,1)} custom-call(bf16[4,4,4,640]{3,2,1,0:T(4,128)(2,1)} %bitcast.16), custom_call_target="tpu_custom_call" | custom-call | flops 60000002048 | bytes 4000000 | tf_op jit(solution)/shard_map/spread/pallas_call | solution.py:72
  33.4 7.6 %all-to-all-start.1 = ((bf16[16,4,16,640]{3,2,1,0:T(8,128)(2,1)}), bf16[16,4,16,640]{3,2,1,0:T(8,128)(2,1)S(1)}, u32[]{:S(2)}, u32[]{:S(2)}) async-start(bf16[16,4,16,640]{3,2,1,0:T(8,128)(2,1)} %spread.1), calls=%async_computation.1 | async-start | bytes 2621440 | tf_op jit(solution)/shard_map/all_to_all | solution.py:400
  41.0 2.9 %collective-permute-start.1 = (bf16[256,640]{1,0:T(8,128)(2,1)S(1)}, bf16[256,640]{1,0:T(8,128)(2,1)S(1)}, u32[]{:S(2)}, u32[]{:S(2)}) collective-permute-start(bf16[256,640]{1,0:T(8,128)(2,1)S(1)} %copy-done.5), channel_id=1, source_target_pairs={{0,2},{2,0},{4,6},{6,4},{1,3},{3,1},{5,7},{7,5},{8,10},{10,8},{12,... | collective-permute-start | bytes 983048 | tf_op jit(solution)/shard_map/ppermute | solution.py:38
  43.9 1.9 %collective-permute-start = (bf16[144,256]{1,0:T(8,128)(2,1)S(1)}, bf16[144,256]{1,0:T(8,128)(2,1)S(1)}, u32[]{:S(2)}, u32[]{:S(2)}) collective-permute-start(bf16[144,256]{1,0:T(8,128)(2,1)S(1)} %bitcast.18), channel_id=1, source_target_pairs={{0,1},{1,0},{2,3},{3,2},{4,5},{5,4},{6,7},{7,6},{8,9},{9,8},{10,11... | collective-permute-start | bytes 221192 | tf_op jit(solution)/shard_map/ppermute | solution.py:34
  46.5 2.6 %pick.1 = bf16[4,144,640]{2,1,0:T(8,128)(2,1)} custom-call(s32[3]{0:T(128)} %pad_add_fusion.place, bf16[144,5120]{1,0:T(8,128)(2,1)} %bitcast.13), custom_call_target="tpu_custom_call" | custom-call | flops 1000000000 | bytes 4000000 | tf_op jit(solution)/shard_map/pick/pallas_call | solution.py:98
  49.1 2.4 %collective-permute-start.4 = (bf16[4,144,640]{2,1,0:T(8,128)(2,1)}, bf16[4,144,640]{2,1,0:T(8,128)(2,1)S(1)}, u32[]{:S(2)}, u32[]{:S(2)}) collective-permute-start(bf16[4,144,640]{2,1,0:T(8,128)(2,1)} %pick.1), channel_id=1, source_target_pairs={{0,1},{1,0},{2,3},{3,2},{4,5},{5,4},{6,7},{7,6},{8,9},{9,8},{10,11... | collective-permute-start | bytes 2211848 | tf_op jit(solution)/shard_map/ppermute | solution.py:34
  55.2 4.9 %accumulate.1.total = bf16[4,2,288,640]{3,2,1,0:T(8,128)(2,1)} custom-call(s32[3]{0:T(128)} %pad_add_fusion.place, bf16[144,256]{1,0:T(8,128)(2,1)} %bitcast.17, bf16[144,256]{1,0:T(8,128)(2,1)} %copy-done.13, bf16[256,640]{1,0:T(8,128)(2,1)} %first.1, bf16[256,640]{1,0:T(8,128)(2,1)} %copy-done.8, bf16[256,640]{1,0:T(8,128)(2,1)} %copy-done.6, ...), custom_call_target="tpu_custom_call" | custom-call | flops 1000000000 | bytes 4000000 | tf_op jit(solution)/shard_map/accumulate/pallas_call | solution.py:153
  61.2 4.4 %project.1 = (bf16[2,256,144]{2,1,0:T(8,128)(2,1)}, f32[2,144,256]{2,1,0:T(8,128)}) custom-call(s32[3]{0:T(128)} %pad_add_fusion.place, bf16[4,2,288,640]{3,2,1,0:T(8,128)(2,1)} %accumulate.1.total, bf16[16,4,16,640]{3,2,1,0:T(8,128)(2,1)} %copy-done), custom_call_target="tpu_custom_call" | custom-call | flops 1000000000 | bytes 4000000 | tf_op jit(solution)/shard_map/project/pallas_call | solution.py:199
  65.6 1.9 %collective-permute-start.5 = (f32[2,144,256]{2,1,0:T(8,128)}, f32[2,144,256]{2,1,0:T(8,128)S(1)}, u32[]{:S(2)}, u32[]{:S(2)}) collective-permute-start(f32[2,144,256]{2,1,0:T(8,128)} %get-tuple-element.22.sums), channel_id=1, source_target_pairs={{0,1},{1,0},{2,3},{3,2},{4,5},{5,4},{6,7},{7,6},{8,9},{9,8},{10,11... | collective-permute-start | bytes 884744 | tf_op jit(solution)/shard_map/ppermute | solution.py:34
  67.5 7.5 %all-to-all-start.2 = ((bf16[32,16,144]{2,1,0:T(8,128)(2,1)}), bf16[32,16,144]{2,1,0:T(8,128)(2,1)S(1)}, u32[]{:S(2)}, u32[]{:S(2)}) async-start(bf16[32,16,144]{2,1,0:T(8,128)(2,1)} %bitcast.15), calls=%async_computation.2 | async-start | bytes 524288 | tf_op jit(solution)/shard_map/all_to_all | solution.py:409
  75.7 4.7 %feedback.1 = (bf16[4,144,640]{2,1,0:T(8,128)(2,1)}, bf16[4,144,640]{2,1,0:T(8,128)(2,1)}) custom-call(s32[3]{0:T(128)} %pad_add_fusion.place, bf16[4,2,288,640]{3,2,1,0:T(8,128)(2,1)} %accumulate.1.total, f32[2,144,256]{2,1,0:T(8,128)} %get-tuple-element.22.sums, f32[2,144,256]{2,1,0:T(8,128)} %copy-done.15, bf16[16,4,16,640]{3,2,1,0:T(8,128)(2,1)} %copy-done), custom_call_target="tpu_custom_call" | custom-call | flops 10000000000 | bytes 4000000 | tf_op jit(solution)/shard_map/feedback/pallas_call | solution.py:248
  80.4 2.7 %all-to-all-done.2.part = bf16[32,16,144]{2,1,0:T(8,128)(2,1)S(1)} async-done(((bf16[32,16,144]{2,1,0:T(8,128)(2,1)}), bf16[32,16,144]{2,1,0:T(8,128)(2,1)S(1)}, u32[]{:S(2)}, u32[]{:S(2)}) %all-to-all-start.2) | async-done | bytes 147488 | tf_op jit(solution)/shard_map/all_to_all | solution.py:409
  85.6 8.7 %all-to-all-start.3 = ((f32[4,24,144]{2,1,0:T(8,128)}), f32[4,24,144]{2,1,0:T(8,128)S(1)}, u32[]{:S(2)}, u32[]{:S(2)}) async-start(f32[4,24,144]{2,1,0:T(8,128)} %combine.1), calls=%async_computation.3 | async-start | bytes 196608 | tf_op jit(solution)/shard_map/all_to_all | solution.py:416
  94.3 1.9 %collective-permute-start.6 = (bf16[4,144,640]{2,1,0:T(8,128)(2,1)S(1)}, bf16[4,144,640]{2,1,0:T(8,128)(2,1)}, u32[]{:S(2)}, u32[]{:S(2)}) collective-permute-start(bf16[4,144,640]{2,1,0:T(8,128)(2,1)S(1)} %copy-done.14), channel_id=1, source_target_pairs={{0,1},{1,0},{2,3},{3,2},{4,5},{5,4},{6,7},{7,6},{8,9},{9,8},{10,11... | collective-permute-start | bytes 2211848 | tf_op jit(solution)/shard_map/ppermute | solution.py:34
  96.2 2.4 %collective-permute-start.7 = (bf16[16,4,16,640]{3,2,1,0:T(8,128)(2,1)S(1)}, bf16[16,4,16,640]{3,2,1,0:T(8,128)(2,1)S(1)}, u32[]{:S(2)}, u32[]{:S(2)}) collective-permute-start(bf16[16,4,16,640]{3,2,1,0:T(8,128)(2,1)S(1)} %copy-done.1), channel_id=1, source_target_pairs={{0,1},{1,0},{2,3},{3,2},{4,5},{5,4},{6,7},{7,6},{8,9},{9,8},{10,11... | collective-permute-start | bytes 3932168 | tf_op jit(solution)/shard_map/ppermute | solution.py:34
  98.7 10.8 %all-to-all-done.3.both = f32[4,24,144]{2,1,0:T(8,128)S(1)} async-done(((f32[4,24,144]{2,1,0:T(8,128)}), f32[4,24,144]{2,1,0:T(8,128)S(1)}, u32[]{:S(2)}, u32[]{:S(2)}) %all-to-all-start.3) | async-done | bytes 55328 | tf_op jit(solution)/shard_map/all_to_all | solution.py:416
  111.7 4.8 %all-to-all-start.4 = ((bf16[16,16,144]{2,1,0:T(8,128)(2,1)}), bf16[16,16,144]{2,1,0:T(8,128)(2,1)S(1)}, u32[]{:S(2)}, u32[]{:S(2)}) async-start(bf16[16,16,144]{2,1,0:T(8,128)(2,1)} %get-tuple-element.26), calls=%async_computation.4 | async-start | bytes 262144 | tf_op jit(solution)/shard_map/all_to_all | solution.py:420
  116.5 3.3 %merge.1 = bf16[144,5120]{1,0:T(8,128)(2,1)} custom-call(s32[3]{0:T(128)} %pad_add_fusion.place, bf16[4,144,640]{2,1,0:T(8,128)(2,1)} %get-tuple-element.30.kept, bf16[4,144,640]{2,1,0:T(8,128)(2,1)} %collective-permute-done.6.received), custom_call_target="tpu_custom_call" | custom-call | flops 3000000000 | bytes 4000000 | tf_op jit(solution)/shard_map/merge/pallas_call | solution.py:291
  119.8 3.1 %all-to-all-done.4.updates = bf16[16,16,144]{2,1,0:T(8,128)(2,1)S(1)} async-done(((bf16[16,16,144]{2,1,0:T(8,128)(2,1)}), bf16[16,16,144]{2,1,0:T(8,128)(2,1)S(1)}, u32[]{:S(2)}, u32[]{:S(2)}) %all-to-all-start.4) | async-done | bytes 73760 | tf_op jit(solution)/shard_map/all_to_all | solution.py:420
  123.6 4.5 %weight_step.1 = bf16[144,5120]{1,0:T(8,128)(2,1)} custom-call(s32[3]{0:T(128)} %pad_add_fusion.place, bf16[16,16,144]{2,1,0:T(8,128)(2,1)} %copy-done.4, bf16[16,4,16,640]{3,2,1,0:T(8,128)(2,1)} %copy-done, bf16[16,4,16,640]{3,2,1,0:T(8,128)(2,1)} %copy-done.2), custom_call_target="tpu_custom_call" | custom-call | flops 1000000000 | bytes 4000000 | tf_op jit(solution)/shard_map/weight_step/pallas_call | solution.py:325
  (46 shorter events, 13.5 us)
Async XLA Ops:
  2.0 28.7 %all-to-all-start = ((bf16[16,4,640]{2,1,0:T(4,128)(2,1)}), bf16[16,4,640]{2,1,0:T(4,128)(2,1)S(1)}, u32[]{:S(2)}, u32[]{:S(2)}) async-start(bf16[16,4,640]{2,1,0:T(4,128)(2,1)} %broadcast_in_dim.4), calls=%async_computation | async-start | bytes 163840 | tf_op jit(solution)/shard_map/all_to_all | solution.py:30
  17.2 34.3 %collective-permute-start.2 = (bf16[256,640]{1,0:T(8,128)(2,1)}, bf16[256,640]{1,0:T(8,128)(2,1)S(1)}, u32[]{:S(2)}, u32[]{:S(2)}) collective-permute-start(bf16[256,640]{1,0:T(8,128)(2,1)} %first.1), channel_id=1, source_target_pairs={{0,4},{2,6},{4,0},{6,2},{1,5},{3,7},{5,1},{7,3},{8,12},{10,14},{12... | collective-permute-start | bytes 983048 | tf_op jit(solution)/shard_map/ppermute | solution.py:38
  21.9 29.6 %collective-permute-start.3 = (bf16[256,640]{1,0:T(8,128)(2,1)}, bf16[256,640]{1,0:T(8,128)(2,1)S(1)}, u32[]{:S(2)}, u32[]{:S(2)}) collective-permute-start(bf16[256,640]{1,0:T(8,128)(2,1)} %first.1), channel_id=1, source_target_pairs={{0,6},{2,4},{4,2},{6,0},{1,7},{3,5},{5,3},{7,1},{8,14},{10,12},{12... | collective-permute-start | bytes 983048 | tf_op jit(solution)/shard_map/ppermute | solution.py:38
  33.4 7.6 %copy-start.5 = (bf16[256,640]{1,0:T(8,128)(2,1)S(1)}, bf16[256,640]{1,0:T(8,128)(2,1)}, u32[]{:S(2)}) copy-start(bf16[256,640]{1,0:T(8,128)(2,1)} %first.1) | copy-start | bytes 983044
  33.4 10.5 %copy-start.12 = (bf16[256,144]{0,1:T(8,128)(2,1)S(1)}, bf16[256,144]{0,1:T(8,128)(2,1)}, u32[]{:S(2)}) copy-start(bf16[256,144]{0,1:T(8,128)(2,1)} %param.6) | copy-start | bytes 221188
  33.4 26.7 %all-to-all-start.1 = ((bf16[16,4,16,640]{3,2,1,0:T(8,128)(2,1)}), bf16[16,4,16,640]{3,2,1,0:T(8,128)(2,1)S(1)}, u32[]{:S(2)}, u32[]{:S(2)}) async-start(bf16[16,4,16,640]{3,2,1,0:T(8,128)(2,1)} %spread.1), calls=%async_computation.1 | async-start | bytes 2621440 | tf_op jit(solution)/shard_map/all_to_all | solution.py:400
  41.0 12.6 %collective-permute-start.1 = (bf16[256,640]{1,0:T(8,128)(2,1)S(1)}, bf16[256,640]{1,0:T(8,128)(2,1)S(1)}, u32[]{:S(2)}, u32[]{:S(2)}) collective-permute-start(bf16[256,640]{1,0:T(8,128)(2,1)S(1)} %copy-done.5), channel_id=1, source_target_pairs={{0,2},{2,0},{4,6},{6,4},{1,3},{3,1},{5,7},{7,5},{8,10},{10,8},{12,... | collective-permute-start | bytes 983048 | tf_op jit(solution)/shard_map/ppermute | solution.py:38
  43.9 9.7 %collective-permute-start = (bf16[144,256]{1,0:T(8,128)(2,1)S(1)}, bf16[144,256]{1,0:T(8,128)(2,1)S(1)}, u32[]{:S(2)}, u32[]{:S(2)}) collective-permute-start(bf16[144,256]{1,0:T(8,128)(2,1)S(1)} %bitcast.18), channel_id=1, source_target_pairs={{0,1},{1,0},{2,3},{3,2},{4,5},{5,4},{6,7},{7,6},{8,9},{9,8},{10,11... | collective-permute-start | bytes 221192 | tf_op jit(solution)/shard_map/ppermute | solution.py:34
  49.1 4.5 %collective-permute-start.4 = (bf16[4,144,640]{2,1,0:T(8,128)(2,1)}, bf16[4,144,640]{2,1,0:T(8,128)(2,1)S(1)}, u32[]{:S(2)}, u32[]{:S(2)}) collective-permute-start(bf16[4,144,640]{2,1,0:T(8,128)(2,1)} %pick.1), channel_id=1, source_target_pairs={{0,1},{1,0},{2,3},{3,2},{4,5},{5,4},{6,7},{7,6},{8,9},{9,8},{10,11... | collective-permute-start | bytes 2211848 | tf_op jit(solution)/shard_map/ppermute | solution.py:34
  51.5 0.7 copy-start.6
  52.3 0.7 copy-start.7
  53.6 0.8 copy-start.8
  54.3 0.9 copy-start.3
  60.1 1.1 copy-start
  65.6 9.4 %collective-permute-start.5 = (f32[2,144,256]{2,1,0:T(8,128)}, f32[2,144,256]{2,1,0:T(8,128)S(1)}, u32[]{:S(2)}, u32[]{:S(2)}) collective-permute-start(f32[2,144,256]{2,1,0:T(8,128)} %get-tuple-element.22.sums), channel_id=1, source_target_pairs={{0,1},{1,0},{2,3},{3,2},{4,5},{5,4},{6,7},{7,6},{8,9},{9,8},{10,11... | collective-permute-start | bytes 884744 | tf_op jit(solution)/shard_map/ppermute | solution.py:34
  67.5 15.6 %all-to-all-start.2 = ((bf16[32,16,144]{2,1,0:T(8,128)(2,1)}), bf16[32,16,144]{2,1,0:T(8,128)(2,1)S(1)}, u32[]{:S(2)}, u32[]{:S(2)}) async-start(bf16[32,16,144]{2,1,0:T(8,128)(2,1)} %bitcast.15), calls=%async_computation.2 | async-start | bytes 524288 | tf_op jit(solution)/shard_map/all_to_all | solution.py:409
  75.0 0.7 copy-start.15
  83.8 10.5 %copy-start.14 = (bf16[4,144,640]{2,1,0:T(8,128)(2,1)S(1)}, bf16[4,144,640]{2,1,0:T(8,128)(2,1)}, u32[]{:S(2)}) copy-start(bf16[4,144,640]{2,1,0:T(8,128)(2,1)} %get-tuple-element.27) | copy-start | bytes 2211844
  83.8 12.4 %copy-start.1 = (bf16[16,4,16,640]{3,2,1,0:T(8,128)(2,1)S(1)}, bf16[16,4,16,640]{3,2,1,0:T(8,128)(2,1)}, u32[]{:S(2)}) copy-start(bf16[16,4,16,640]{3,2,1,0:T(8,128)(2,1)} %copy-done) | copy-start | bytes 3932164
  85.6 23.9 %all-to-all-start.3 = ((f32[4,24,144]{2,1,0:T(8,128)}), f32[4,24,144]{2,1,0:T(8,128)S(1)}, u32[]{:S(2)}, u32[]{:S(2)}) async-start(f32[4,24,144]{2,1,0:T(8,128)} %combine.1), calls=%async_computation.3 | async-start | bytes 196608 | tf_op jit(solution)/shard_map/all_to_all | solution.py:416
  94.3 22.2 %collective-permute-start.6 = (bf16[4,144,640]{2,1,0:T(8,128)(2,1)S(1)}, bf16[4,144,640]{2,1,0:T(8,128)(2,1)}, u32[]{:S(2)}, u32[]{:S(2)}) collective-permute-start(bf16[4,144,640]{2,1,0:T(8,128)(2,1)S(1)} %copy-done.14), channel_id=1, source_target_pairs={{0,1},{1,0},{2,3},{3,2},{4,5},{5,4},{6,7},{7,6},{8,9},{9,8},{10,11... | collective-permute-start | bytes 2211848 | tf_op jit(solution)/shard_map/ppermute | solution.py:34
  96.2 20.3 %collective-permute-start.7 = (bf16[16,4,16,640]{3,2,1,0:T(8,128)(2,1)S(1)}, bf16[16,4,16,640]{3,2,1,0:T(8,128)(2,1)S(1)}, u32[]{:S(2)}, u32[]{:S(2)}) collective-permute-start(bf16[16,4,16,640]{3,2,1,0:T(8,128)(2,1)S(1)} %copy-done.1), channel_id=1, source_target_pairs={{0,1},{1,0},{2,3},{3,2},{4,5},{5,4},{6,7},{7,6},{8,9},{9,8},{10,11... | collective-permute-start | bytes 3932168 | tf_op jit(solution)/shard_map/ppermute | solution.py:34
  111.7 11.3 %all-to-all-start.4 = ((bf16[16,16,144]{2,1,0:T(8,128)(2,1)}), bf16[16,16,144]{2,1,0:T(8,128)(2,1)S(1)}, u32[]{:S(2)}, u32[]{:S(2)}) async-start(bf16[16,16,144]{2,1,0:T(8,128)(2,1)} %get-tuple-element.26), calls=%async_computation.4 | async-start | bytes 262144 | tf_op jit(solution)/shard_map/all_to_all | solution.py:420
  116.5 3.3 %copy-start.2 = (bf16[16,4,16,640]{3,2,1,0:T(8,128)(2,1)}, bf16[16,4,16,640]{3,2,1,0:T(8,128)(2,1)S(1)}, u32[]{:S(2)}) copy-start(bf16[16,4,16,640]{3,2,1,0:T(8,128)(2,1)S(1)} %collective-permute-done.7.other) | copy-start | bytes 3932164
  (5 other events, 3.3 us)

commit v2 on v1

v2 whole, which is shorter than its diff:
```python
import jax
import jax.numpy as jnp
from jax import lax
from jax.experimental import pallas as pl
from jax.experimental.pallas import tpu as pltpu
from jax.sharding import Mesh, PartitionSpec as P

STEP = 20
BETA_ONE = 0.9
BETA_TWO = 0.999
EPSILON = 1e-08

AXES = ("zh", "x", "y", "zl", "c")
SIZES = (4, 4, 4, 4, 2)
DP = ("zh", "x", "y")
TENSOR = ("zl", "c")
ROWS, WIDTH, RANK, TOKENS = 144, 640, 256, 256
COLUMNS = 8 * WIDTH
LIMITS = {"project": 50, "feedback": 60, "weight_step": 24, "merge": 60}
LONG = 60_000_000_000
SHORT = 1_000_000_000
LONG_MERGE = 3_000_000_000
LONG_UPDATE = 17_000_000_000
LONG_FEEDBACK = 10_000_000_000
LONG_GRADIENTS = 10_300_000_000
f32, bf16 = jnp.float32, jnp.bfloat16


def to_all(block, axes, size):
    return lax.all_to_all(jnp.broadcast_to(block[None], (size, *block.shape)), axes, 0, 0)


def swap_cores(block):
    return lax.ppermute(block, "c", [(0, 1), (1, 0)])


def from_xor(block, bits):
    return lax.ppermute(block, "zl", [(i, i ^ bits) for i in range(4)])


def halves(value):
    high = value.astype(bf16)
    return high, (value - high.astype(f32)).astype(bf16)


def call(kernel, name, out_shape, in_specs, out_specs, scratch, cycles):
    return pl.pallas_call(
        kernel,
        out_shape=out_shape,
        in_specs=in_specs,
        out_specs=out_specs,
        scratch_shapes=scratch,
        compiler_params=pltpu.CompilerParams(vmem_limit_bytes=LIMITS.get(name, 8) * 1024 * 1024),
        cost_estimate=pl.CostEstimate(flops=cycles, bytes_accessed=4_000_000, transcendentals=0),
        name=name,
    )


VM, SM, ANY = pl.BlockSpec(memory_space=pltpu.VMEM), pl.BlockSpec(memory_space=pltpu.SMEM), pl.BlockSpec(memory_space=pl.ANY)
CONTRACT = (((1,), (1,)), ((), ()))
BASIS = (16, 4, 16, WIDTH)


def spread_kernel(along_z, out):
    for zl in range(4):
        block = jnp.concatenate([along_z[zh, zl].astype(f32) for zh in range(4)], axis=0).astype(bf16)
        for peer in range(16):
            out[peer, zl] = block


def spread(along_z):
    return call(
        spread_kernel, "spread", jax.ShapeDtypeStruct(BASIS, bf16), [VM], VM, [], LONG
    )(along_z)


def pick_kernel(place, error, act, out, held, sems, done):
    copies, outs = [], []
    for z in range(4):
        start = pl.multiple_of((2 * z + 1 - place[1]) * WIDTH, 128)
        copies.append(pltpu.make_async_copy(error.at[:, pl.ds(start, WIDTH)], held.at[z], sems.at[z]))
    copies.append(pltpu.make_async_copy(act, held.at[4, :, pl.ds(0, TOKENS)], sems.at[4]))
    for copy in copies:
        copy.start()
    held[4, :, TOKENS:] = jnp.zeros((ROWS, WIDTH - TOKENS), bf16)
    for z in range(5):
        copies[z].wait()
        outs.append(pltpu.make_async_copy(held.at[z], out.at[z], done.at[z]))
        outs[z].start()
    for copy in outs:
        copy.wait()


def pick(place, error, act):
    shape = jax.ShapeDtypeStruct((5, ROWS, WIDTH), bf16)
    scratch = [
        pltpu.VMEM((5, ROWS, WIDTH), bf16),
        pltpu.SemaphoreType.DMA((5,)),
        pltpu.SemaphoreType.DMA((5,)),
    ]
    return call(pick_kernel, "pick", shape, [SM, ANY, ANY], ANY, scratch, SHORT)(place, error, act)


def arrived_kernel(first, second, out):
    out[...] = jnp.zeros_like(out)


def arrived(first, second):
    shape = jax.ShapeDtypeStruct((8, 128), f32)
    return call(arrived_kernel, "arrived", shape, [ANY, ANY], VM, [], LONG_GRADIENTS)(first, second)


def start_basis(source, target, sems):
    copies = [pltpu.make_async_copy(source.at[pl.ds(4 * i, 4)], target.at[pl.ds(4 * i, 4)], sems.at[i]) for i in range(4)]
    for copy in copies:
        copy.start()
    return copies


def project_kernel(
    place, act, picked, first, second, third, fourth, error, own, ready, turned, sums, total,
    acts, grads, errors, basis, totals, sems, basis_sems, act_sems, done,
):
    zl, core = place[0], place[1]
    heads = [
        pltpu.make_async_copy(act, acts.at[0], act_sems.at[0]),
        pltpu.make_async_copy(picked.at[4, :, pl.ds(0, TOKENS)], acts.at[1], act_sems.at[1]),
    ]
    for copy in heads:
        copy.start()
    copies = []
    for bits, source in enumerate((first, second, third, fourth)):
        z = zl ^ bits
        start = pl.multiple_of((2 * z + core) * WIDTH, 128)
        moved = [
            pltpu.make_async_copy(source, grads.at[bits], sems.at[bits, 0]),
            pltpu.make_async_copy(error.at[:, pl.ds(start, WIDTH)], errors.at[0, bits], sems.at[bits, 1]),
            pltpu.make_async_copy(picked.at[z], errors.at[1, bits], sems.at[bits, 2]),
        ]
        for copy in moved:
            copy.start()
        copies.append(moved)
    halves_of_basis = start_basis(own, basis, basis_sems)
    for copy in heads:
        copy.wait()
    outs = []
    for bits in range(4):
        for copy in copies[bits]:
            copy.wait()
        for side in range(2):
            gradient = jnp.dot(acts[side], grads[bits], preferred_element_type=f32).astype(bf16)
            high, low = halves(gradient.astype(f32) + errors[side, bits].astype(f32))
            totals[bits, side, :ROWS] = high
            totals[bits, side, ROWS:] = low
            outs.append(pltpu.make_async_copy(totals.at[bits, side], total.at[zl ^ bits, side], done.at[bits, side]))
            outs[-1].start()
    for copy in halves_of_basis:
        copy.wait()
    values = [jnp.zeros((2 * ROWS, RANK), f32)] * 2
    for bits in range(4):
        part = basis[:, zl ^ bits].reshape(RANK, WIDTH)
        for side in range(2):
            values[side] += lax.dot_general(totals[bits, side], part, CONTRACT, preferred_element_type=f32)
    for side in range(2):
        projected = values[side][:ROWS] + values[side][ROWS:]
        sums[side] = projected
        padded = jnp.concatenate([projected, jnp.zeros((RANK - ROWS, RANK), f32)], axis=0)
        turned[1 - core if side else core] = padded.T[:, :ROWS].astype(bf16)
    for copy in outs:
        copy.wait()


def project(place, act, picked, grads, error, own, ready):
    return call(
        project_kernel,
        "project",
        (
            jax.ShapeDtypeStruct((2, RANK, ROWS), bf16),
            jax.ShapeDtypeStruct((2, ROWS, RANK), f32),
            jax.ShapeDtypeStruct((4, 2, 2 * ROWS, WIDTH), bf16),
        ),
        [SM] + [ANY] * 8 + [VM],
        (VM, VM, ANY),
        [
            pltpu.VMEM((2, ROWS, TOKENS), bf16),
            pltpu.VMEM((4, TOKENS, WIDTH), bf16),
            pltpu.VMEM((2, 4, ROWS, WIDTH), bf16),
            pltpu.VMEM(BASIS, bf16),
            pltpu.VMEM((4, 2, 2 * ROWS, WIDTH), bf16),
            pltpu.SemaphoreType.DMA((4, 3)),
            pltpu.SemaphoreType.DMA((4,)),
            pltpu.SemaphoreType.DMA((2,)),
            pltpu.SemaphoreType.DMA((4, 2)),
        ],
        SHORT,
    )(place, act, picked, *grads, error, own, ready)


def feedback_kernel(total, sums, received, own, kept, sent, totals, basis, results, sems, basis_sems, done):
    halves_of_basis = start_basis(own, basis, basis_sems)
    copies = [pltpu.make_async_copy(total.at[z], totals.at[z], sems.at[z]) for z in range(4)]
    for copy in copies:
        copy.start()
    backs = []
    for side in range(2):
        backs.append(jnp.concatenate(halves(sums[side] + received[1 - side]), axis=0))
    for copy in halves_of_basis:
        copy.wait()
    outs = []
    for z in range(4):
        copies[z].wait()
        part = basis[:, z].reshape(RANK, WIDTH)
        for side, target in ((1, sent), (0, kept)):
            back = jnp.dot(backs[side], part, preferred_element_type=f32)
            value = totals[z, side, :ROWS].astype(f32) + totals[z, side, ROWS:].astype(f32)
            results[side, z] = (value - (back[:ROWS] + back[ROWS:])).astype(bf16)
            outs.append(pltpu.make_async_copy(results.at[side, z], target.at[z], done.at[side, z]))
            outs[-1].start()
    for copy in outs:
        copy.wait()


def feedback(total, sums, received, own):
    shape = jax.ShapeDtypeStruct((4, ROWS, WIDTH), bf16)
    return call(
        feedback_kernel,
        "feedback",
        (shape, shape),
        [ANY, VM, VM, ANY],
        (ANY, ANY),
        [
            pltpu.VMEM((4, 2, 2 * ROWS, WIDTH), bf16),
            pltpu.VMEM(BASIS, bf16),
            pltpu.VMEM((2, 4, ROWS, WIDTH), bf16),
            pltpu.SemaphoreType.DMA((4,)),
            pltpu.SemaphoreType.DMA((4,)),
            pltpu.SemaphoreType.DMA((2, 4)),
        ],
        LONG_FEEDBACK,
    )(total, sums, received, own)


def merge_kernel(place, kept, received, out, held, sems, done):
    core = place[1]
    copies, outs = [], []
    for z in range(4):
        for side, source in enumerate((kept, received)):
            start = pl.multiple_of((2 * z + (1 - core if side else core)) * WIDTH, 128)
            copies.append(pltpu.make_async_copy(source.at[z], held.at[:, pl.ds(start, WIDTH)], sems.at[z, side]))
            copies[-1].start()
    for copy in copies:
        copy.wait()
    for part in range(3):
        rows = pl.ds(part * 48, 48)
        outs.append(pltpu.make_async_copy(held.at[rows], out.at[rows], done.at[part]))
        outs[part].start()
    for copy in outs:
        copy.wait()


def merge(place, kept, received):
    shape = jax.ShapeDtypeStruct((ROWS, COLUMNS), bf16)
    scratch = [
        pltpu.VMEM((ROWS, COLUMNS), bf16),
        pltpu.SemaphoreType.DMA((4, 2)),
        pltpu.SemaphoreType.DMA((3,)),
    ]
    return call(merge_kernel, "merge", shape, [SM, ANY, ANY], ANY, scratch, LONG_MERGE)(place, kept, received)


def weight_kernel(place, updates, own, other, out, held, mine, theirs, results, head, sems, done):
    first = place[1] == 0
    head_copy = pltpu.make_async_copy(updates, held, head.at[0])
    head_copy.start()
    copies = start_basis(own, mine, sems.at[0]) + start_basis(other, theirs, sems.at[1])
    head_copy.wait()
    value = held[...].reshape(RANK, ROWS).astype(f32)
    padded = jnp.concatenate([value, jnp.zeros((RANK, RANK - ROWS), f32)], axis=1)
    turned = padded.T[:ROWS].astype(bf16)
    for copy in copies:
        copy.wait()
    outs = []
    for z in range(4):
        both = mine[:, z].reshape(RANK, WIDTH), theirs[:, z].reshape(RANK, WIDTH)
        for core in range(2):
            part = jnp.where(first, both[core], both[1 - core])
            start = (2 * z + core) * WIDTH
            step = jnp.dot(turned, part, preferred_element_type=f32)
            results[:, start : start + WIDTH] = step.astype(bf16)
        columns = pl.ds(z * 2 * WIDTH, 2 * WIDTH)
        outs.append(pltpu.make_async_copy(results.at[:, columns], out.at[:, columns], done.at[z]))
        outs[z].start()
    for copy in outs:
        copy.wait()


def weight(place, updates, own, other):
    return call(
        weight_kernel,
        "weight_step",
        jax.ShapeDtypeStruct((ROWS, COLUMNS), bf16),
        [SM, ANY, ANY, ANY],
        ANY,
        [
            pltpu.VMEM((16, 16, ROWS), bf16),
            pltpu.VMEM(BASIS, bf16),
            pltpu.VMEM(BASIS, bf16),
            pltpu.VMEM((ROWS, COLUMNS), bf16),
            pltpu.SemaphoreType.DMA((1,)),
            pltpu.SemaphoreType.DMA((2, 4)),
            pltpu.SemaphoreType.DMA((4,)),
        ],
        SHORT,
    )(place, updates, own, other)


def combine_kernel(part, first, second, out):
    total = jnp.sum(part[...].astype(f32), axis=0)
    for peer in range(4):
        out[peer, :16] = total
        out[peer, 16:20] = first[...]
        out[peer, 20:] = second[...]


def combine(part, first, second):
    shape = jax.ShapeDtypeStruct((4, 24, ROWS), f32)
    return call(combine_kernel, "combine", shape, [VM] * 3, VM, [], SHORT)(part, first, second)


def moments(first, second, mean):
    first = BETA_ONE * first + (1.0 - BETA_ONE) * mean
    second = BETA_TWO * second + (1.0 - BETA_TWO) * mean * mean
    return first, second


def update_kernel(place, both, out, first_own, second_own, held):
    mean = (both[0, :16] + both[1, :16] + both[2, :16] + both[3, :16]) / 64
    for peer in range(4):
        held[peer] = mean[4 * peer : 4 * peer + 4]
    first = jnp.concatenate([both[peer, 16:20] for peer in range(4)], axis=0)
    second = jnp.concatenate([both[peer, 20:24] for peer in range(4)], axis=0)
    first, second = moments(first, second, mean)
    first_hat = first / (1.0 - BETA_ONE**STEP)
    second_hat = second / (1.0 - BETA_TWO**STEP)
    update = (first_hat / (jnp.sqrt(second_hat) + EPSILON)).astype(bf16)
    for peer in range(16):
        out[peer] = update
    zh = place[2]
    mine = held[zh]
    first_own[...], second_own[...] = moments(both[zh, 16:20], both[zh, 20:24], mine)


def new_update(place, both):
    shape = jax.ShapeDtypeStruct((4, ROWS), f32)
    return call(
        update_kernel,
        "update",
        (jax.ShapeDtypeStruct((16, 16, ROWS), bf16), shape, shape),
        [SM, VM],
        (VM, VM, VM),
        [pltpu.VMEM((4, 4, ROWS), f32)],
        LONG_UPDATE,
    )(place, both)


def local(hidden_act, out_grad, error_in, subspace, first_moment, second_moment):
    zh = lax.axis_index("zh")
    place = jnp.stack([lax.axis_index("zl"), lax.axis_index("c"), zh]).astype(jnp.int32)
    act = hidden_act.T

    along_z = to_all(subspace.T, ("zh", "zl"), 16)
    spreading = spread(along_z.reshape(4, 4, 4, WIDTH))
    own = lax.all_to_all(spreading, ("x", "y"), 0, 0)
    error = error_in[0]
    error = error_in[0]
    grads = [out_grad] + [from_xor(out_grad, bits) for bits in (1, 2, 3)]
    picked = swap_cores(pick(place, error, act))
    ready = arrived(grads[2], grads[3])
    own, ready, picked, grads[1] = lax.optimization_barrier((own, ready, picked, grads[1]))
    turned, sums, total = project(place, act, picked, grads, error, own, ready)

    part = lax.all_to_all(turned.reshape(32, 16, ROWS), ("c", "x", "y"), 0, 0)
    received = swap_cores(sums)
    error_kept, error_sent = feedback(total, sums, received, own)
    part, error_kept, error_sent, later = lax.optimization_barrier((part, error_kept, error_sent, own))
    other = swap_cores(later)
    error_received = swap_cores(error_sent)
    both = combine(part, first_moment.T, second_moment.T)
    both = lax.all_to_all(both, "zh", 0, 0)
    error_received, other = lax.optimization_barrier((error_received, other))
    error_out = merge(place, error_kept, error_received)
    update, first_own, second_own = new_update(place, both)
    updates = lax.all_to_all(update, ("x", "y"), 0, 0)
    weight_step = weight(place, updates, own, other)
    return (weight_step, error_out[None], first_own.T, second_own.T)


def solution(mesh):
    fine = Mesh(mesh.devices.reshape(SIZES), AXES)
    placed = (
        P(DP, TENSOR),
        P(DP, TENSOR),
        P(DP, TENSOR, None),
        P(TENSOR, DP),
        P(TENSOR, DP),
        P(TENSOR, DP),
    )
    return jax.shard_map(
        local,
        mesh=fine,
        in_specs=placed,
        out_specs=(P(TENSOR, None), P(DP, TENSOR, None), P(TENSOR, DP), P(TENSOR, DP)),
        check_vma=False,
    )
```

time: 129 us -> 118 us (0.915)
  Pallas kernels: 30.4 us -> 21.6 us
  waiting for transfers between devices: 22.1 us -> 29.5 us
  starting transfers between devices: 65.3 us -> 60.6 us
  local copies, waits for them, and re-layouts: 8.83 us -> 4.21 us
    ppermute x3, waiting for transfers between devices: 0.01 us -> 9.22 us  [from_xor(): return lax.ppermute(block, 'zl', [(i, i ^ bits) for i in range(4)])]
    pallas_call x3 -> x2, Pallas kernels: 12.1 us -> 7.38 us  [the longest x1 5.42 us: feedback(): call(feedback_kernel, 'feedback', (shape, shape), [ANY, VM, VM, ANY], (AN...]
    unnamed x32 -> x26, local copies, waits for them, and re-layouts: 7.48 us -> 2.86 us
    ppermute x5 -> x4, starting transfers between devices: 10.6 us -> 8.16 us  [swap_cores(): return lax.ppermute(block, 'c', [(0, 1), (1, 0)])]
    all_to_all x1, starting transfers between devices: 8.69 us -> 6.32 us  [local(): both = lax.all_to_all(both, 'zh', 0, 0)]
    pallas_call x1, Pallas kernels: 2.1 us -> 0.15 us  [spread(): call(spread_kernel, 'spread', jax.ShapeDtypeStruct(BASIS, bf16), [VM], VM...]
    all_to_all x1, waiting for transfers between devices: 10.8 us -> 9.17 us  [local(): both = lax.all_to_all(both, 'zh', 0, 0)]
    pallas_call x1, Pallas kernels: 4.49 us -> 3.19 us  [weight(): call(weight_kernel, 'weight_step', jax.ShapeDtypeStruct((ROWS, COLUMNS),...]
  transfers between devices with their start and end apart: 13 -> 12, of which waited for: 4 -> 7; matrix products, arithmetic and copies ran while one was open for 1% -> 0% of each run, Pallas kernels for 15% -> 10%
where the time goes in v2:
time: 118 us; the launch traced here: 117 us
  starting transfers between devices  60.6 us (51%)
  waiting for transfers between devices  29.5 us (25%)
  Pallas kernels  21.6 us (18%)
  local copies, waits for them, and re-layouts  4.21 us (4%)
    all_to_all x1, starting transfers between devices, to_all(): lax.all_to_all(jnp.broadcast_to(block[None], (size, *block.shape)), axes,...  15.2 us
    ppermute x3, starting transfers between devices, from_xor(): return lax.ppermute(block, 'zl', [(i, i ^ bits) for i in range(4)])  10.4 us
    ppermute x3, waiting for transfers between devices, from_xor(): return lax.ppermute(block, 'zl', [(i, i ^ bits) for i in range(4)])  9.22 us
    all_to_all x1, waiting for transfers between devices, local(): both = lax.all_to_all(both, 'zh', 0, 0)  9.17 us
    ppermute x4, starting transfers between devices, swap_cores(): return lax.ppermute(block, 'c', [(0, 1), (1, 0)])  8.16 us
    all_to_all x1, starting transfers between devices, local(): own = lax.all_to_all(spreading, ('x', 'y'), 0, 0)  7.61 us
    all_to_all x1, starting transfers between devices, local(): part = lax.all_to_all(turned.reshape(32, 16, ROWS), ('c', 'x', 'y'), 0, 0)  7.26 us
    all_to_all x1, starting transfers between devices, local(): both = lax.all_to_all(both, 'zh', 0, 0)  6.32 us
  transfers between devices with their start and end apart: 12, of which 7 were waited for; matrix products, arithmetic and copies ran while one was open for 0% of the time, Pallas kernels for 10%

profile of v2, /device:TPU:2, one launch (start us, length us, event | category | flops | bytes accessed | tf_op | source)
XLA Modules:
  0.0 116.8 jit_solution(14508107520831588735)
XLA Ops:
  0.6 1.3 %broadcast_in_dim.4 = bf16[16,4,640]{2,1,0:T(4,128)(2,1)} broadcast(bf16[4,640]{1,0:T(4,128)(2,1)} %bitcast.20), dimensions={1,2} | broadcast | bytes 87040 | tf_op jit(solution)/shard_map/broadcast_in_dim | solution.py:30
  2.0 15.2 %all-to-all-start = ((bf16[16,4,640]{2,1,0:T(4,128)(2,1)}), bf16[16,4,640]{2,1,0:T(4,128)(2,1)S(1)}, u32[]{:S(2)}, u32[]{:S(2)}) async-start(bf16[16,4,640]{2,1,0:T(4,128)(2,1)} %broadcast_in_dim.4), calls=%async_computation | async-start | bytes 163840 | tf_op jit(solution)/shard_map/all_to_all | solution.py:30
  17.2 5.6 %collective-permute-start.1 = (bf16[256,640]{1,0:T(8,128)(2,1)}, bf16[256,640]{1,0:T(8,128)(2,1)S(1)}, u32[]{:S(2)}, u32[]{:S(2)}) collective-permute-start(bf16[256,640]{1,0:T(8,128)(2,1)} %first.1), channel_id=1, source_target_pairs={{0,6},{2,4},{4,2},{6,0},{1,7},{3,5},{5,3},{7,1},{8,14},{10,12},{12... | collective-permute-start | bytes 983048 | tf_op jit(solution)/shard_map/ppermute | solution.py:38
  22.8 1.9 %collective-permute-start = (bf16[256,640]{1,0:T(8,128)(2,1)}, bf16[256,640]{1,0:T(8,128)(2,1)}, u32[]{:S(2)}, u32[]{:S(2)}) collective-permute-start(bf16[256,640]{1,0:T(8,128)(2,1)} %first.1), channel_id=1, source_target_pairs={{0,4},{2,6},{4,0},{6,2},{1,5},{3,7},{5,1},{7,3},{8,12},{10,14},{12... | collective-permute-start | bytes 983048 | tf_op jit(solution)/shard_map/ppermute | solution.py:38
  24.7 5.9 %all-to-all-done = bf16[16,4,640]{2,1,0:T(4,128)(2,1)S(1)} async-done(((bf16[16,4,640]{2,1,0:T(4,128)(2,1)}), bf16[16,4,640]{2,1,0:T(4,128)(2,1)S(1)}, u32[]{:S(2)}, u32[]{:S(2)}) %all-to-all-start) | async-done | bytes 81952 | tf_op jit(solution)/shard_map/all_to_all | solution.py:30
  31.9 7.6 %all-to-all-start.1 = ((bf16[16,4,16,640]{3,2,1,0:T(8,128)(2,1)}), bf16[16,4,16,640]{3,2,1,0:T(8,128)(2,1)S(1)}, u32[]{:S(2)}, u32[]{:S(2)}) async-start(bf16[16,4,16,640]{3,2,1,0:T(8,128)(2,1)} %copy-done.3), calls=%async_computation.1 | async-start | bytes 2621440 | tf_op jit(solution)/shard_map/all_to_all | solution.py:373
  39.5 2.9 %collective-permute-start.3 = (bf16[256,640]{1,0:T(8,128)(2,1)S(1)}, bf16[256,640]{1,0:T(8,128)(2,1)}, u32[]{:S(2)}, u32[]{:S(2)}) collective-permute-start(bf16[256,640]{1,0:T(8,128)(2,1)S(1)} %copy-done.4), channel_id=1, source_target_pairs={{0,2},{2,0},{4,6},{6,4},{1,3},{3,1},{5,7},{7,5},{8,10},{10,8},{12,... | collective-permute-start | bytes 983048 | tf_op jit(solution)/shard_map/ppermute | solution.py:38
  42.5 2.0 %pick.1 = bf16[5,144,640]{2,1,0:T(8,128)(2,1)S(1)} custom-call(s32[3]{0:T(128)S(1)} %pad_add_fusion.place, bf16[144,5120]{1,0:T(8,128)(2,1)S(1)} %bitcast.14, bf16[144,256]{1,0:T(8,128)(2,1)S(1)} %bitcast.16), custom_call_target="tpu_custom_call" | custom-call | flops 1000000000 | bytes 4000000 | tf_op jit(solution)/shard_map/pick/pallas_call | solution.py:101
  44.4 1.9 %collective-permute-start.2 = (bf16[5,144,640]{2,1,0:T(8,128)(2,1)S(1)}, bf16[5,144,640]{2,1,0:T(8,128)(2,1)S(1)}, u32[]{:S(2)}, u32[]{:S(2)}) collective-permute-start(bf16[5,144,640]{2,1,0:T(8,128)(2,1)S(1)} %pick.1), channel_id=1, source_target_pairs={{0,1},{1,0},{2,3},{3,2},{4,5},{5,4},{6,7},{7,6},{8,9},{9,8},{10,11... | collective-permute-start | bytes 2764808 | tf_op jit(solution)/shard_map/ppermute | solution.py:34
  46.4 6.8 %collective-permute-done.first.third = bf16[256,640]{1,0:T(8,128)(2,1)} collective-permute-done((bf16[256,640]{1,0:T(8,128)(2,1)}, bf16[256,640]{1,0:T(8,128)(2,1)}, u32[]{:S(2)}, u32[]{:S(2)}) %collective-permute-start) | collective-permute-done | bytes 327712 | tf_op jit(solution)/shard_map/ppermute | solution.py:38
  53.2 2.4 %collective-permute-done.3.second = bf16[256,640]{1,0:T(8,128)(2,1)} collective-permute-done((bf16[256,640]{1,0:T(8,128)(2,1)S(1)}, bf16[256,640]{1,0:T(8,128)(2,1)}, u32[]{:S(2)}, u32[]{:S(2)}) %collective-permute-start.3) | collective-permute-done | bytes 327712 | tf_op jit(solution)/shard_map/ppermute | solution.py:38
  56.9 5.6 %project.1 = (bf16[2,256,144]{2,1,0:T(8,128)(2,1)}, f32[2,144,256]{2,1,0:T(8,128)S(1)}, bf16[4,2,288,640]{3,2,1,0:T(8,128)(2,1)}) custom-call(s32[3]{0:T(128)S(1)} %pad_add_fusion.place, bf16[144,256]{1,0:T(8,128)(2,1)S(1)} %bitcast.17, bf16[5,144,640]{2,1,0:T(8,128)(2,1)S(1)} %collective-permute-done.2.picked, bf16[256,640]{1,0:T(8,128)(2,1)S(1)} %copy-done.4, ...), custom_call_target="tpu_custom_call" | custom-call | flops 1000000000 | bytes 4000000 | tf_op jit(solution)/shard_map/project/pallas_call | solution.py:174
  62.5 1.9 %collective-permute-start.4 = (f32[2,144,256]{2,1,0:T(8,128)S(1)}, f32[2,144,256]{2,1,0:T(8,128)S(1)}, u32[]{:S(2)}, u32[]{:S(2)}) collective-permute-start(f32[2,144,256]{2,1,0:T(8,128)S(1)} %get-tuple-element.28.sums), channel_id=1, source_target_pairs={{0,1},{1,0},{2,3},{3,2},{4,5},{5,4},{6,7},{7,6},{8,9},{9,8},{10,11... | collective-permute-start | bytes 884744 | tf_op jit(solution)/shard_map/ppermute | solution.py:34
  64.4 7.3 %all-to-all-start.2 = ((bf16[32,16,144]{2,1,0:T(8,128)(2,1)}), bf16[32,16,144]{2,1,0:T(8,128)(2,1)S(1)}, u32[]{:S(2)}, u32[]{:S(2)}) async-start(bf16[32,16,144]{2,1,0:T(8,128)(2,1)} %bitcast.7), calls=%async_computation.2 | async-start | bytes 524288 | tf_op jit(solution)/shard_map/all_to_all | solution.py:382
  72.4 5.4 %feedback.1 = (bf16[4,144,640]{2,1,0:T(8,128)(2,1)}, bf16[4,144,640]{2,1,0:T(8,128)(2,1)}) custom-call(bf16[4,2,288,640]{3,2,1,0:T(8,128)(2,1)} %get-tuple-element.27.total, f32[2,144,256]{2,1,0:T(8,128)} %copy-done.8, f32[2,144,256]{2,1,0:T(8,128)} %copy-done.12, bf16[16,4,16,640]{3,2,1,0:T(8,128)(2,1)} %copy-done), custom_call_target="tpu_custom_call" | custom-call | flops 10000000000 | bytes 4000000 | tf_op jit(solution)/shard_map/feedback/pallas_call | solution.py:225
  77.8 2.0 %all-to-all-done.2.part = bf16[32,16,144]{2,1,0:T(8,128)(2,1)S(1)} async-done(((bf16[32,16,144]{2,1,0:T(8,128)(2,1)}), bf16[32,16,144]{2,1,0:T(8,128)(2,1)S(1)}, u32[]{:S(2)}, u32[]{:S(2)}) %all-to-all-start.2) | async-done | bytes 147488 | tf_op jit(solution)/shard_map/all_to_all | solution.py:382
  80.5 6.3 %all-to-all-start.3 = ((f32[4,24,144]{2,1,0:T(8,128)}), f32[4,24,144]{2,1,0:T(8,128)S(1)}, u32[]{:S(2)}, u32[]{:S(2)}) async-start(f32[4,24,144]{2,1,0:T(8,128)} %combine.1), calls=%async_computation.3 | async-start | bytes 196608 | tf_op jit(solution)/shard_map/all_to_all | solution.py:389
  86.8 1.9 %collective-permute-start.5 = (bf16[4,144,640]{2,1,0:T(8,128)(2,1)S(1)}, bf16[4,144,640]{2,1,0:T(8,128)(2,1)}, u32[]{:S(2)}, u32[]{:S(2)}) collective-permute-start(bf16[4,144,640]{2,1,0:T(8,128)(2,1)S(1)} %copy-done.11), channel_id=1, source_target_pairs={{0,1},{1,0},{2,3},{3,2},{4,5},{5,4},{6,7},{7,6},{8,9},{9,8},{10,11... | collective-permute-start | bytes 2211848 | tf_op jit(solution)/shard_map/ppermute | solution.py:34
  88.8 2.4 %collective-permute-start.6 = (bf16[16,4,16,640]{3,2,1,0:T(8,128)(2,1)S(1)}, bf16[16,4,16,640]{3,2,1,0:T(8,128)(2,1)S(1)}, u32[]{:S(2)}, u32[]{:S(2)}) collective-permute-start(bf16[16,4,16,640]{3,2,1,0:T(8,128)(2,1)S(1)} %copy-done.1), channel_id=1, source_target_pairs={{0,1},{1,0},{2,3},{3,2},{4,5},{5,4},{6,7},{7,6},{8,9},{9,8},{10,11... | collective-permute-start | bytes 3932168 | tf_op jit(solution)/shard_map/ppermute | solution.py:34
  91.2 9.2 %all-to-all-done.3.both = f32[4,24,144]{2,1,0:T(8,128)S(1)} async-done(((f32[4,24,144]{2,1,0:T(8,128)}), f32[4,24,144]{2,1,0:T(8,128)S(1)}, u32[]{:S(2)}, u32[]{:S(2)}) %all-to-all-start.3) | async-done | bytes 55328 | tf_op jit(solution)/shard_map/all_to_all | solution.py:389
  101.6 5.6 %all-to-all-start.4 = ((bf16[16,16,144]{2,1,0:T(8,128)(2,1)}), bf16[16,16,144]{2,1,0:T(8,128)(2,1)S(1)}, u32[]{:S(2)}, u32[]{:S(2)}) async-start(bf16[16,16,144]{2,1,0:T(8,128)(2,1)} %get-tuple-element.32), calls=%async_computation.4 | async-start | bytes 262144 | tf_op jit(solution)/shard_map/all_to_all | solution.py:393
  107.2 3.3 %merge.1 = bf16[144,5120]{1,0:T(8,128)(2,1)} custom-call(s32[3]{0:T(128)} %copy-done.6, bf16[4,144,640]{2,1,0:T(8,128)(2,1)} %get-tuple-element.36.kept, bf16[4,144,640]{2,1,0:T(8,128)(2,1)} %collective-permute-done.5.received), custom_call_target="tpu_custom_call" | custom-call | flops 3000000000 | bytes 4000000 | tf_op jit(solution)/shard_map/merge/pallas_call | solution.py:268
  110.5 3.0 %all-to-all-done.4.updates = bf16[16,16,144]{2,1,0:T(8,128)(2,1)S(1)} async-done(((bf16[16,16,144]{2,1,0:T(8,128)(2,1)}), bf16[16,16,144]{2,1,0:T(8,128)(2,1)S(1)}, u32[]{:S(2)}, u32[]{:S(2)}) %all-to-all-start.4) | async-done | bytes 73760 | tf_op jit(solution)/shard_map/all_to_all | solution.py:393
  113.6 3.2 %weight_step.1 = bf16[144,5120]{1,0:T(8,128)(2,1)} custom-call(s32[3]{0:T(128)S(1)} %copy-done.7, bf16[16,16,144]{2,1,0:T(8,128)(2,1)S(1)} %all-to-all-done.4.updates, bf16[16,4,16,640]{3,2,1,0:T(8,128)(2,1)S(1)} %copy-done.1, bf16[16,4,16,640]{3,2,1,0:T(8,128)(2,1)S(1)} %collective-permute-done.6.other), custom_call_target="tpu_custom_call" | custom-call | flops 1000000000 | bytes 4000000 | tf_op jit(solution)/shard_map/weight_step/pallas_call | solution.py:298
  (37 shorter events, 5.2 us)
Async XLA Ops:
  2.0 28.7 %all-to-all-start = ((bf16[16,4,640]{2,1,0:T(4,128)(2,1)}), bf16[16,4,640]{2,1,0:T(4,128)(2,1)S(1)}, u32[]{:S(2)}, u32[]{:S(2)}) async-start(bf16[16,4,640]{2,1,0:T(4,128)(2,1)} %broadcast_in_dim.4), calls=%async_computation | async-start | bytes 163840 | tf_op jit(solution)/shard_map/all_to_all | solution.py:30
  17.2 29.2 %collective-permute-start.1 = (bf16[256,640]{1,0:T(8,128)(2,1)}, bf16[256,640]{1,0:T(8,128)(2,1)S(1)}, u32[]{:S(2)}, u32[]{:S(2)}) collective-permute-start(bf16[256,640]{1,0:T(8,128)(2,1)} %first.1), channel_id=1, source_target_pairs={{0,6},{2,4},{4,2},{6,0},{1,7},{3,5},{5,3},{7,1},{8,14},{10,12},{12... | collective-permute-start | bytes 983048 | tf_op jit(solution)/shard_map/ppermute | solution.py:38
  22.8 30.4 %collective-permute-start = (bf16[256,640]{1,0:T(8,128)(2,1)}, bf16[256,640]{1,0:T(8,128)(2,1)}, u32[]{:S(2)}, u32[]{:S(2)}) collective-permute-start(bf16[256,640]{1,0:T(8,128)(2,1)} %first.1), channel_id=1, source_target_pairs={{0,4},{2,6},{4,0},{6,2},{1,5},{3,7},{5,1},{7,3},{8,12},{10,14},{12... | collective-permute-start | bytes 983048 | tf_op jit(solution)/shard_map/ppermute | solution.py:38
  30.8 1.1 copy-start.3
  31.9 7.6 %copy-start.4 = (bf16[256,640]{1,0:T(8,128)(2,1)S(1)}, bf16[256,640]{1,0:T(8,128)(2,1)}, u32[]{:S(2)}) copy-start(bf16[256,640]{1,0:T(8,128)(2,1)} %first.1) | copy-start | bytes 983044
  31.9 10.6 %copy-start.2 = (bf16[1,144,5120]{2,1,0:T(8,128)(2,1)S(1)}, bf16[1,144,5120]{2,1,0:T(8,128)(2,1)}, u32[]{:S(2)}) copy-start(bf16[1,144,5120]{2,1,0:T(8,128)(2,1)} %param.8) | copy-start | bytes 4423684
  31.9 10.6 %copy-start.5 = (bf16[256,144]{0,1:T(8,128)(2,1)S(1)}, bf16[256,144]{0,1:T(8,128)(2,1)}, u32[]{:S(2)}) copy-start(bf16[256,144]{0,1:T(8,128)(2,1)} %param.6) | copy-start | bytes 221188
  31.9 23.9 %all-to-all-start.1 = ((bf16[16,4,16,640]{3,2,1,0:T(8,128)(2,1)}), bf16[16,4,16,640]{3,2,1,0:T(8,128)(2,1)S(1)}, u32[]{:S(2)}, u32[]{:S(2)}) async-start(bf16[16,4,16,640]{3,2,1,0:T(8,128)(2,1)} %copy-done.3), calls=%async_computation.1 | async-start | bytes 2621440 | tf_op jit(solution)/shard_map/all_to_all | solution.py:373
  39.5 16.1 %collective-permute-start.3 = (bf16[256,640]{1,0:T(8,128)(2,1)S(1)}, bf16[256,640]{1,0:T(8,128)(2,1)}, u32[]{:S(2)}, u32[]{:S(2)}) collective-permute-start(bf16[256,640]{1,0:T(8,128)(2,1)S(1)} %copy-done.4), channel_id=1, source_target_pairs={{0,2},{2,0},{4,6},{6,4},{1,3},{3,1},{5,7},{7,5},{8,10},{10,8},{12,... | collective-permute-start | bytes 983048 | tf_op jit(solution)/shard_map/ppermute | solution.py:38
  42.4 57.9 %copy-start.6 = (s32[3]{0:T(128)}, s32[3]{0:T(128)S(1)}, u32[]{:S(2)}) copy-start(s32[3]{0:T(128)S(1)} %pad_add_fusion.place) | copy-start | bytes 40
  44.4 11.2 %collective-permute-start.2 = (bf16[5,144,640]{2,1,0:T(8,128)(2,1)S(1)}, bf16[5,144,640]{2,1,0:T(8,128)(2,1)S(1)}, u32[]{:S(2)}, u32[]{:S(2)}) collective-permute-start(bf16[5,144,640]{2,1,0:T(8,128)(2,1)S(1)} %pick.1), channel_id=1, source_target_pairs={{0,1},{1,0},{2,3},{3,2},{4,5},{5,4},{6,7},{7,6},{8,9},{9,8},{10,11... | collective-permute-start | bytes 2764808 | tf_op jit(solution)/shard_map/ppermute | solution.py:34
  55.8 1.1 copy-start
  62.5 9.2 %copy-start.8 = (f32[2,144,256]{2,1,0:T(8,128)}, f32[2,144,256]{2,1,0:T(8,128)S(1)}, u32[]{:S(2)}) copy-start(f32[2,144,256]{2,1,0:T(8,128)S(1)} %get-tuple-element.28.sums) | copy-start | bytes 884740
  62.5 9.2 %collective-permute-start.4 = (f32[2,144,256]{2,1,0:T(8,128)S(1)}, f32[2,144,256]{2,1,0:T(8,128)S(1)}, u32[]{:S(2)}, u32[]{:S(2)}) collective-permute-start(f32[2,144,256]{2,1,0:T(8,128)S(1)} %get-tuple-element.28.sums), channel_id=1, source_target_pairs={{0,1},{1,0},{2,3},{3,2},{4,5},{5,4},{6,7},{7,6},{8,9},{9,8},{10,11... | collective-permute-start | bytes 884744 | tf_op jit(solution)/shard_map/ppermute | solution.py:34
  64.4 15.4 %all-to-all-start.2 = ((bf16[32,16,144]{2,1,0:T(8,128)(2,1)}), bf16[32,16,144]{2,1,0:T(8,128)(2,1)S(1)}, u32[]{:S(2)}, u32[]{:S(2)}) async-start(bf16[32,16,144]{2,1,0:T(8,128)(2,1)} %bitcast.7), calls=%async_computation.2 | async-start | bytes 524288 | tf_op jit(solution)/shard_map/all_to_all | solution.py:382
  72.4 7.4 %copy-start.9 = (f32[144,4]{0,1:T(4,128)S(1)}, f32[144,4]{0,1:T(4,128)}, u32[]{:S(2)}) copy-start(f32[144,4]{0,1:T(4,128)} %param.10) | copy-start | bytes 6916
  72.4 7.4 %copy-start.10 = (f32[144,4]{0,1:T(4,128)S(1)}, f32[144,4]{0,1:T(4,128)}, u32[]{:S(2)}) copy-start(f32[144,4]{0,1:T(4,128)} %param.11) | copy-start | bytes 6916
  79.8 7.0 %copy-start.11 = (bf16[4,144,640]{2,1,0:T(8,128)(2,1)S(1)}, bf16[4,144,640]{2,1,0:T(8,128)(2,1)}, u32[]{:S(2)}) copy-start(bf16[4,144,640]{2,1,0:T(8,128)(2,1)} %get-tuple-element.33) | copy-start | bytes 2211844
  79.8 8.9 %copy-start.1 = (bf16[16,4,16,640]{3,2,1,0:T(8,128)(2,1)S(1)}, bf16[16,4,16,640]{3,2,1,0:T(8,128)(2,1)}, u32[]{:S(2)}) copy-start(bf16[16,4,16,640]{3,2,1,0:T(8,128)(2,1)} %copy-done) | copy-start | bytes 3932164
  80.5 19.8 %all-to-all-start.3 = ((f32[4,24,144]{2,1,0:T(8,128)}), f32[4,24,144]{2,1,0:T(8,128)S(1)}, u32[]{:S(2)}, u32[]{:S(2)}) async-start(f32[4,24,144]{2,1,0:T(8,128)} %combine.1), calls=%async_computation.3 | async-start | bytes 196608 | tf_op jit(solution)/shard_map/all_to_all | solution.py:389
  86.8 20.3 %collective-permute-start.5 = (bf16[4,144,640]{2,1,0:T(8,128)(2,1)S(1)}, bf16[4,144,640]{2,1,0:T(8,128)(2,1)}, u32[]{:S(2)}, u32[]{:S(2)}) collective-permute-start(bf16[4,144,640]{2,1,0:T(8,128)(2,1)S(1)} %copy-done.11), channel_id=1, source_target_pairs={{0,1},{1,0},{2,3},{3,2},{4,5},{5,4},{6,7},{7,6},{8,9},{9,8},{10,11... | collective-permute-start | bytes 2211848 | tf_op jit(solution)/shard_map/ppermute | solution.py:34
  88.8 18.4 %collective-permute-start.6 = (bf16[16,4,16,640]{3,2,1,0:T(8,128)(2,1)S(1)}, bf16[16,4,16,640]{3,2,1,0:T(8,128)(2,1)S(1)}, u32[]{:S(2)}, u32[]{:S(2)}) collective-permute-start(bf16[16,4,16,640]{3,2,1,0:T(8,128)(2,1)S(1)} %copy-done.1), channel_id=1, source_target_pairs={{0,1},{1,0},{2,3},{3,2},{4,5},{5,4},{6,7},{7,6},{8,9},{9,8},{10,11... | collective-permute-start | bytes 3932168 | tf_op jit(solution)/shard_map/ppermute | solution.py:34
  101.6 12.0 %all-to-all-start.4 = ((bf16[16,16,144]{2,1,0:T(8,128)(2,1)}), bf16[16,16,144]{2,1,0:T(8,128)(2,1)S(1)}, u32[]{:S(2)}, u32[]{:S(2)}) async-start(bf16[16,16,144]{2,1,0:T(8,128)(2,1)} %get-tuple-element.32), calls=%async_computation.4 | async-start | bytes 262144 | tf_op jit(solution)/shard_map/all_to_all | solution.py:393
  107.2 6.4 %copy-start.7 = (s32[3]{0:T(128)S(1)}, s32[3]{0:T(128)}, u32[]{:S(2)}) copy-start(s32[3]{0:T(128)} %copy-done.6) | copy-start | bytes 40
  (1 other events, 0.7 us)

commit v3 on v2

--- a/solution.py
+++ b/solution.py
@@ -1,3 +1,5 @@
+import functools
+
 import jax
 import jax.numpy as jnp
 from jax import lax
@@ -16,18 +18,14 @@
 TENSOR = ("zl", "c")
 ROWS, WIDTH, RANK, TOKENS = 144, 640, 256, 256
 COLUMNS = 8 * WIDTH
-LIMITS = {"project": 50, "feedback": 60, "weight_step": 24, "merge": 60}
+LIMITS = {"project": 50, "feedback": 50, "weight_step": 24}
 LONG = 60_000_000_000
 SHORT = 1_000_000_000
-LONG_MERGE = 3_000_000_000
-LONG_UPDATE = 17_000_000_000
-LONG_FEEDBACK = 10_000_000_000
+LONG_COMBINE = 17_000_000_000
+LONG_UPDATE = 1_000_000_000
+LONG_FEEDBACK = 1_000_000_000
 LONG_GRADIENTS = 10_300_000_000
 f32, bf16 = jnp.float32, jnp.bfloat16
-
-
-def to_all(block, axes, size):
-    return lax.all_to_all(jnp.broadcast_to(block[None], (size, *block.shape)), axes, 0, 0)
 
 
 def swap_cores(block):
@@ -59,6 +57,16 @@
 VM, SM, ANY = pl.BlockSpec(memory_space=pltpu.VMEM), pl.BlockSpec(memory_space=pltpu.SMEM), pl.BlockSpec(memory_space=pl.ANY)
 CONTRACT = (((1,), (1,)), ((), ()))
 BASIS = (16, 4, 16, WIDTH)
+
+
+def repeat_kernel(block, out):
+    for peer in range(16):
+        out[peer] = block[...]
+
+
+def repeat(block):
+    shape = jax.ShapeDtypeStruct((16, *block.shape), bf16)
+    return call(repeat_kernel, "repeat", shape, [VM], VM, [], SHORT)(block)
 
 
 def spread_kernel(along_z, out):
@@ -118,7 +126,7 @@
 
 
 def project_kernel(
-    place, act, picked, first, second, third, fourth, error, own, ready, turned, sums, total,
+    place, act, picked, first, second, third, fourth, error, own, ready, turned, sums, sums_sent, total, total_sent,
     acts, grads, errors, basis, totals, sems, basis_sems, act_sems, done,
 ):
     zl, core = place[0], place[1]
@@ -152,7 +160,8 @@
             high, low = halves(gradient.astype(f32) + errors[side, bits].astype(f32))
             totals[bits, side, :ROWS] = high
             totals[bits, side, ROWS:] = low
-            outs.append(pltpu.make_async_copy(totals.at[bits, side], total.at[zl ^ bits, side], done.at[bits, side]))
+            target = (total_sent if side else total).at[zl ^ bits]
+            outs.append(pltpu.make_async_copy(totals.at[bits, side], target, done.at[bits, side]))
             outs[-1].start()
     for copy in halves_of_basis:
         copy.wait()
@@ -163,7 +172,7 @@
             values[side] += lax.dot_general(totals[bits, side], part, CONTRACT, preferred_element_type=f32)
     for side in range(2):
         projected = values[side][:ROWS] + values[side][ROWS:]
-        sums[side] = projected
+        (sums_sent if side else sums)[...] = projected
         padded = jnp.concatenate([projected, jnp.zeros((RANK - ROWS, RANK), f32)], axis=0)
         turned[1 - core if side else core] = padded.T[:, :ROWS].astype(bf16)
     for copy in outs:
@@ -176,11 +185,13 @@
         "project",
         (
             jax.ShapeDtypeStruct((2, RANK, ROWS), bf16),
-            jax.ShapeDtypeStruct((2, ROWS, RANK), f32),
-            jax.ShapeDtypeStruct((4, 2, 2 * ROWS, WIDTH), bf16),
+            jax.ShapeDtypeStruct((ROWS, RANK), f32),
+            jax.ShapeDtypeStruct((ROWS, RANK), f32),
+            jax.ShapeDtypeStruct((4, 2 * ROWS, WIDTH), bf16),
+            jax.ShapeDtypeStruct((4, 2 * ROWS, WIDTH), bf16),
         ),
         [SM] + [ANY] * 8 + [VM],
-        (VM, VM, ANY),
+        (VM, VM, VM, ANY, ANY),
         [
             pltpu.VMEM((2, ROWS, TOKENS), bf16),
             pltpu.VMEM((4, TOKENS, WIDTH), bf16),
@@ -196,76 +207,64 @@
     )(place, act, picked, *grads, error, own, ready)
 
 
-def feedback_kernel(total, sums, received, own, kept, sent, totals, basis, results, sems, basis_sems, done):
-    halves_of_basis = start_basis(own, basis, basis_sems)
-    copies = [pltpu.make_async_copy(total.at[z], totals.at[z], sems.at[z]) for z in range(4)]
+def feedback_kernel(
+    blocks, place, total, total_other, sums, received, own, other, *rest
+):
+    out, totals, basis, results, sems, basis_sems, done = rest[-7:]
+    core = place[1]
+    copies, moved = [], []
+    for side, source in enumerate((own, other)):
+        for i in range(4):
+            peers = pl.ds(4 * i, 4)
+            half = source.at[peers, pl.ds(blocks[0], 2)]
+            copies.append(pltpu.make_async_copy(half, basis.at[side, peers], basis_sems.at[side, i]))
+            copies[-1].start()
+    for i, z in enumerate(blocks):
+        for side, source in enumerate((total, total_other)):
+            moved.append(pltpu.make_async_copy(source.at[z], totals.at[i, side], sems.at[i, side]))
+            moved[-1].start()
+    backs = jnp.concatenate(halves(sums[...] + received[...]), axis=0)
     for copy in copies:
-        copy.start()
-    backs = []
-    for side in range(2):
-        backs.append(jnp.concatenate(halves(sums[side] + received[1 - side]), axis=0))
-    for copy in halves_of_basis:
         copy.wait()
     outs = []
-    for z in range(4):
-        copies[z].wait()
-        part = basis[:, z].reshape(RANK, WIDTH)
-        for side, target in ((1, sent), (0, kept)):
-            back = jnp.dot(backs[side], part, preferred_element_type=f32)
-            value = totals[z, side, :ROWS].astype(f32) + totals[z, side, ROWS:].astype(f32)
-            results[side, z] = (value - (back[:ROWS] + back[ROWS:])).astype(bf16)
-            outs.append(pltpu.make_async_copy(results.at[side, z], target.at[z], done.at[side, z]))
+    for i, z in enumerate(blocks):
+        for side in range(2):
+            moved[2 * i + side].wait()
+            part = basis[side, :, i].reshape(RANK, WIDTH)
+            back = jnp.dot(backs, part, preferred_element_type=f32)
+            value = totals[i, side, :ROWS].astype(f32) + totals[i, side, ROWS:].astype(f32)
+            results[i, side] = (value - (back[:ROWS] + back[ROWS:])).astype(bf16)
+            start = pl.multiple_of((2 * z + (1 - core if side else core)) * WIDTH, 128)
+            outs.append(pltpu.make_async_copy(results.at[i, side], out.at[:, pl.ds(start, WIDTH)], done.at[i, side]))
             outs[-1].start()
     for copy in outs:
         copy.wait()
 
 
-def feedback(total, sums, received, own):
-    shape = jax.ShapeDtypeStruct((4, ROWS, WIDTH), bf16)
-    return call(
-        feedback_kernel,
-        "feedback",
-        (shape, shape),
-        [ANY, VM, VM, ANY],
-        (ANY, ANY),
-        [
-            pltpu.VMEM((4, 2, 2 * ROWS, WIDTH), bf16),
-            pltpu.VMEM(BASIS, bf16),
-            pltpu.VMEM((2, 4, ROWS, WIDTH), bf16),
-            pltpu.SemaphoreType.DMA((4,)),
-            pltpu.SemaphoreType.DMA((4,)),
+def feedback(blocks, begun, place, total, total_other, sums, received, own, other):
+    operands = (place, total, total_other, sums, received, own, other)
+    in_specs = [SM, ANY, ANY, VM, VM, ANY, ANY]
+    aliases = {}
+    if begun is not None:
+        operands, in_specs, aliases = (*operands, begun), in_specs + [ANY], {7: 0}
+    return pl.pallas_call(
+        functools.partial(feedback_kernel, blocks),
+        out_shape=jax.ShapeDtypeStruct((ROWS, COLUMNS), bf16),
+        in_specs=in_specs,
+        out_specs=ANY,
+        scratch_shapes=[
+            pltpu.VMEM((2, 2, 2 * ROWS, WIDTH), bf16),
+            pltpu.VMEM((2, 16, 2, 16, WIDTH), bf16),
+            pltpu.VMEM((2, 2, ROWS, WIDTH), bf16),
+            pltpu.SemaphoreType.DMA((2, 2)),
             pltpu.SemaphoreType.DMA((2, 4)),
+            pltpu.SemaphoreType.DMA((2, 2)),
         ],
-        LONG_FEEDBACK,
-    )(total, sums, received, own)
-
-
-def merge_kernel(place, kept, received, out, held, sems, done):
-    core = place[1]
-    copies, outs = [], []
-    for z in range(4):
-        for side, source in enumerate((kept, received)):
-            start = pl.multiple_of((2 * z + (1 - core if side else core)) * WIDTH, 128)
-            copies.append(pltpu.make_async_copy(source.at[z], held.at[:, pl.ds(start, WIDTH)], sems.at[z, side]))
-            copies[-1].start()
-    for copy in copies:
-        copy.wait()
-    for part in range(3):
-        rows = pl.ds(part * 48, 48)
-        outs.append(pltpu.make_async_copy(held.at[rows], out.at[rows], done.at[part]))
-        outs[part].start()
-    for copy in outs:
-        copy.wait()
-
-
-def merge(place, kept, received):
-    shape = jax.ShapeDtypeStruct((ROWS, COLUMNS), bf16)
-    scratch = [
-        pltpu.VMEM((ROWS, COLUMNS), bf16),
-        pltpu.SemaphoreType.DMA((4, 2)),
-        pltpu.SemaphoreType.DMA((3,)),
-    ]
-    return call(merge_kernel, "merge", shape, [SM, ANY, ANY], ANY, scratch, LONG_MERGE)(place, kept, received)
+        input_output_aliases=aliases,
+        compiler_params=pltpu.CompilerParams(vmem_limit_bytes=LIMITS["feedback"] * 1024 * 1024),
+        cost_estimate=pl.CostEstimate(flops=LONG_FEEDBACK, bytes_accessed=4_000_000, transcendentals=0),
+        name="feedback",
+    )(*operands)
 
 
 def weight_kernel(place, updates, own, other, out, held, mine, theirs, results, head, sems, done):
@@ -324,7 +323,7 @@
 
 def combine(part, first, second):
     shape = jax.ShapeDtypeStruct((4, 24, ROWS), f32)
-    return call(combine_kernel, "combine", shape, [VM] * 3, VM, [], SHORT)(part, first, second)
+    return call(combine_kernel, "combine", shape, [VM] * 3, VM, [], LONG_COMBINE)(part, first, second)
 
 
 def moments(first, second, mean):
@@ -368,7 +367,7 @@
     place = jnp.stack([lax.axis_index("zl"), lax.axis_index("c"), zh]).astype(jnp.int32)
     act = hidden_act.T
 
-    along_z = to_all(subspace.T, ("zh", "zl"), 16)
+    along_z = lax.all_to_all(repeat(subspace.T), ("zh", "zl"), 0, 0)
     spreading = spread(along_z.reshape(4, 4, 4, WIDTH))
     own = lax.all_to_all(spreading, ("x", "y"), 0, 0)
     error = error_in[0]
@@ -377,18 +376,16 @@
     picked = swap_cores(pick(place, error, act))
     ready = arrived(grads[2], grads[3])
     own, ready, picked, grads[1] = lax.optimization_barrier((own, ready, picked, grads[1]))
-    turned, sums, total = project(place, act, picked, grads, error, own, ready)
+    turned, sums, sums_sent, total, total_sent = project(place, act, picked, grads, error, own, ready)
 
     part = lax.all_to_all(turned.reshape(32, 16, ROWS), ("c", "x", "y"), 0, 0)
-    received = swap_cores(sums)
-    error_kept, error_sent = feedback(total, sums, received, own)
-    part, error_kept, error_sent, later = lax.optimization_barrier((part, error_kept, error_sent, own))
-    other = swap_cores(later)
-    error_received = swap_cores(error_sent)
+    received, total_other, other = swap_cores(sums_sent), swap_cores(total_sent), swap_cores(own)
     both = combine(part, first_moment.T, second_moment.T)
     both = lax.all_to_all(both, "zh", 0, 0)
-    error_received, other = lax.optimization_barrier((error_received, other))
-    error_out = merge(place, error_kept, error_received)
+    needed = place, total, total_other, sums, received, own, other
+    begun = feedback((0, 1), None, *needed)
+    both, begun = lax.optimization_barrier((both, begun))
+    error_out = feedback((2, 3), begun, *needed)
     update, first_own, second_own = new_update(place, both)
     updates = lax.all_to_all(update, ("x", "y"), 0, 0)
     weight_step = weight(place, updates, own, other)

time: 118 us -> 116 us (0.983)
  local copies, waits for them, and re-layouts: 4.21 us -> 2.82 us
    broadcast_in_dim x1 -> x0, local copies, waits for them, and re-layouts: 1.35 us -> none  [to_all(): jnp.broadcast_to(block[None], (size, *block.shape))]
    pallas_call x3 -> x4, Pallas kernels: 9.44 us -> 9.39 us  [the longest x2 8.05 us: feedback(): pl.pallas_call(functools.partial(feedback_kernel, blocks), out_shape=jax....]
    unnamed x26 -> x18, local copies, waits for them, and re-layouts: 2.86 us -> 2.82 us
  transfers between devices with their start and end apart: 12 -> 12, of which waited for: 7 -> 7; matrix products, arithmetic and copies ran while one was open for 0% -> 0% of each run, Pallas kernels for 10% -> 9%
where the time goes in v3:
time: 116 us; the launch traced here: 115 us
  starting transfers between devices  60.8 us (52%)
  waiting for transfers between devices  29 us (25%)
  Pallas kernels  21.5 us (19%)
  local copies, waits for them, and re-layouts  2.82 us (2%)
    all_to_all x1, starting transfers between devices, local(): along_z = lax.all_to_all(repeat(subspace.T), ('zh', 'zl'), 0, 0)  15.2 us
    ppermute x3, starting transfers between devices, from_xor(): return lax.ppermute(block, 'zl', [(i, i ^ bits) for i in range(4)])  10.3 us
    all_to_all x1, waiting for transfers between devices, local(): both = lax.all_to_all(both, 'zh', 0, 0)  9.44 us
    ppermute x3, waiting for transfers between devices, from_xor(): return lax.ppermute(block, 'zl', [(i, i ^ bits) for i in range(4)])  9.36 us
    ppermute x4, starting transfers between devices, swap_cores(): return lax.ppermute(block, 'c', [(0, 1), (1, 0)])  8.31 us
    pallas_call x2, Pallas kernels, feedback(): pl.pallas_call(functools.partial(feedback_kernel, blocks), out_shape=jax....  8.05 us
    all_to_all x1, starting transfers between devices, local(): own = lax.all_to_all(spreading, ('x', 'y'), 0, 0)  7.61 us
    all_to_all x1, starting transfers between devices, local(): part = lax.all_to_all(turned.reshape(32, 16, ROWS), ('c', 'x', 'y'), 0, 0)  7.31 us
  transfers between devices with their start and end apart: 12, of which 7 were waited for; matrix products, arithmetic and copies ran while one was open for 0% of the time, Pallas kernels for 9%

profile of v3, /device:TPU:2, one launch (start us, length us, event | category | flops | bytes accessed | tf_op | source)
XLA Modules:
  0.0 115.1 jit_solution(9034691587939761100)
XLA Ops:
  2.0 15.2 %all-to-all-start = ((bf16[16,4,640]{2,1,0:T(4,128)(2,1)}), bf16[16,4,640]{2,1,0:T(4,128)(2,1)S(1)}, u32[]{:S(2)}, u32[]{:S(2)}) async-start(bf16[16,4,640]{2,1,0:T(4,128)(2,1)} %repeat.1), calls=%async_computation | async-start | bytes 163840 | tf_op jit(solution)/shard_map/all_to_all | solution.py:370
  17.2 5.6 %collective-permute-start.1 = (bf16[256,640]{1,0:T(8,128)(2,1)S(1)}, bf16[256,640]{1,0:T(8,128)(2,1)S(1)}, u32[]{:S(2)}, u32[]{:S(2)}) collective-permute-start(bf16[256,640]{1,0:T(8,128)(2,1)S(1)} %copy-done.4), channel_id=1, source_target_pairs={{0,6},{2,4},{4,2},{6,0},{1,7},{3,5},{5,3},{7,1},{8,14},{10,12},{12... | collective-permute-start | bytes 983048 | tf_op jit(solution)/shard_map/ppermute | solution.py:36
  22.8 1.9 %collective-permute-start = (bf16[256,640]{1,0:T(8,128)(2,1)S(1)}, bf16[256,640]{1,0:T(8,128)(2,1)}, u32[]{:S(2)}, u32[]{:S(2)}) collective-permute-start(bf16[256,640]{1,0:T(8,128)(2,1)S(1)} %copy-done.4), channel_id=1, source_target_pairs={{0,4},{2,6},{4,0},{6,2},{1,5},{3,7},{5,1},{7,3},{8,12},{10,14},{12... | collective-permute-start | bytes 983048 | tf_op jit(solution)/shard_map/ppermute | solution.py:36
  24.7 6.0 %all-to-all-done = bf16[16,4,640]{2,1,0:T(4,128)(2,1)S(1)} async-done(((bf16[16,4,640]{2,1,0:T(4,128)(2,1)}), bf16[16,4,640]{2,1,0:T(4,128)(2,1)S(1)}, u32[]{:S(2)}, u32[]{:S(2)}) %all-to-all-start) | async-done | bytes 81952 | tf_op jit(solution)/shard_map/all_to_all | solution.py:370
  32.0 7.6 %all-to-all-start.1 = ((bf16[16,4,16,640]{3,2,1,0:T(8,128)(2,1)}), bf16[16,4,16,640]{3,2,1,0:T(8,128)(2,1)S(1)}, u32[]{:S(2)}, u32[]{:S(2)}) async-start(bf16[16,4,16,640]{3,2,1,0:T(8,128)(2,1)} %copy-done.3), calls=%async_computation.1 | async-start | bytes 2621440 | tf_op jit(solution)/shard_map/all_to_all | solution.py:372
  39.6 2.7 %collective-permute-start.3 = (bf16[256,640]{1,0:T(8,128)(2,1)S(1)}, bf16[256,640]{1,0:T(8,128)(2,1)}, u32[]{:S(2)}, u32[]{:S(2)}) collective-permute-start(bf16[256,640]{1,0:T(8,128)(2,1)S(1)} %copy-done.4), channel_id=1, source_target_pairs={{0,2},{2,0},{4,6},{6,4},{1,3},{3,1},{5,7},{7,5},{8,10},{10,8},{12,... | collective-permute-start | bytes 983048 | tf_op jit(solution)/shard_map/ppermute | solution.py:36
  42.4 2.0 %pick.1 = bf16[5,144,640]{2,1,0:T(8,128)(2,1)S(1)} custom-call(s32[3]{0:T(128)S(1)} %pad_add_fusion.place, bf16[144,5120]{1,0:T(8,128)(2,1)S(1)} %bitcast.14, bf16[144,256]{1,0:T(8,128)(2,1)S(1)} %bitcast.16), custom_call_target="tpu_custom_call" | custom-call | flops 1000000000 | bytes 4000000 | tf_op jit(solution)/shard_map/pick/pallas_call | solution.py:109
  44.4 1.9 %collective-permute-start.2 = (bf16[5,144,640]{2,1,0:T(8,128)(2,1)S(1)}, bf16[5,144,640]{2,1,0:T(8,128)(2,1)S(1)}, u32[]{:S(2)}, u32[]{:S(2)}) collective-permute-start(bf16[5,144,640]{2,1,0:T(8,128)(2,1)S(1)} %pick.1), channel_id=1, source_target_pairs={{0,1},{1,0},{2,3},{3,2},{4,5},{5,4},{6,7},{7,6},{8,9},{9,8},{10,11... | collective-permute-start | bytes 2764808 | tf_op jit(solution)/shard_map/ppermute | solution.py:32
  46.3 6.6 %collective-permute-done.first.third = bf16[256,640]{1,0:T(8,128)(2,1)} collective-permute-done((bf16[256,640]{1,0:T(8,128)(2,1)S(1)}, bf16[256,640]{1,0:T(8,128)(2,1)}, u32[]{:S(2)}, u32[]{:S(2)}) %collective-permute-start) | collective-permute-done | bytes 327712 | tf_op jit(solution)/shard_map/ppermute | solution.py:36
  53.0 2.7 %collective-permute-done.3.second = bf16[256,640]{1,0:T(8,128)(2,1)} collective-permute-done((bf16[256,640]{1,0:T(8,128)(2,1)S(1)}, bf16[256,640]{1,0:T(8,128)(2,1)}, u32[]{:S(2)}, u32[]{:S(2)}) %collective-permute-start.3) | collective-permute-done | bytes 327712 | tf_op jit(solution)/shard_map/ppermute | solution.py:36
  56.9 5.6 %project.1 = (bf16[2,256,144]{2,1,0:T(8,128)(2,1)}, f32[144,256]{1,0:T(8,128)S(1)}, f32[144,256]{1,0:T(8,128)}, bf16[4,288,640]{2,1,0:T(8,128)(2,1)}, bf16[4,288,640]{2,1,0:T(8,128)(2,1)}) custom-call(s32[3]{0:T(128)S(1)} %pad_add_fusion.place, bf16[144,256]{1,0:T(8,128)(2,1)S(1)} %bitcast.17, bf16[5,144,640]{2,1,0:T(8,128)(2,1)S(1)} %collective-permute-done.2.picked, ...), custom_call_target="tpu_custom_call" | custom-call | flops 1000000000 | bytes 4000000 | tf_op jit(solution)/shard_map/project/pallas_call | solution.py:183
  62.5 7.3 %all-to-all-start.2 = ((bf16[32,16,144]{2,1,0:T(8,128)(2,1)}), bf16[32,16,144]{2,1,0:T(8,128)(2,1)S(1)}, u32[]{:S(2)}, u32[]{:S(2)}) async-start(bf16[32,16,144]{2,1,0:T(8,128)(2,1)} %bitcast.7), calls=%async_computation.2 | async-start | bytes 524288 | tf_op jit(solution)/shard_map/all_to_all | solution.py:381
  69.8 2.1 %collective-permute-start.6 = (bf16[16,4,16,640]{3,2,1,0:T(8,128)(2,1)}, bf16[16,4,16,640]{3,2,1,0:T(8,128)(2,1)S(1)}, u32[]{:S(2)}, u32[]{:S(2)}) collective-permute-start(bf16[16,4,16,640]{3,2,1,0:T(8,128)(2,1)} %copy-done), channel_id=1, source_target_pairs={{0,1},{1,0},{2,3},{3,2},{4,5},{5,4},{6,7},{7,6},{8,9},{9,8},{10,11... | collective-permute-start | bytes 3932168 | tf_op jit(solution)/shard_map/ppermute | solution.py:32
  71.9 2.3 %collective-permute-start.5 = (f32[144,256]{1,0:T(8,128)}, f32[144,256]{1,0:T(8,128)S(1)}, u32[]{:S(2)}, u32[]{:S(2)}) collective-permute-start(f32[144,256]{1,0:T(8,128)} %get-tuple-element.26), channel_id=1, source_target_pairs={{0,1},{1,0},{2,3},{3,2},{4,5},{5,4},{6,7},{7,6},{8,9},{9,8},{10,11... | collective-permute-start | bytes 442376 | tf_op jit(solution)/shard_map/ppermute | solution.py:32
  74.1 2.1 %collective-permute-start.4 = (bf16[4,288,640]{2,1,0:T(8,128)(2,1)}, bf16[4,288,640]{2,1,0:T(8,128)(2,1)}, u32[]{:S(2)}, u32[]{:S(2)}) collective-permute-start(bf16[4,288,640]{2,1,0:T(8,128)(2,1)} %get-tuple-element.24), channel_id=1, source_target_pairs={{0,1},{1,0},{2,3},{3,2},{4,5},{5,4},{6,7},{7,6},{8,9},{9,8},{10,11... | collective-permute-start | bytes 4423688 | tf_op jit(solution)/shard_map/ppermute | solution.py:32
  76.2 1.7 %all-to-all-done.2.part = bf16[32,16,144]{2,1,0:T(8,128)(2,1)S(1)} async-done(((bf16[32,16,144]{2,1,0:T(8,128)(2,1)}), bf16[32,16,144]{2,1,0:T(8,128)(2,1)S(1)}, u32[]{:S(2)}, u32[]{:S(2)}) %all-to-all-start.2) | async-done | bytes 147488 | tf_op jit(solution)/shard_map/all_to_all | solution.py:381
  78.6 6.2 %all-to-all-start.3 = ((f32[4,24,144]{2,1,0:T(8,128)}), f32[4,24,144]{2,1,0:T(8,128)S(1)}, u32[]{:S(2)}, u32[]{:S(2)}) async-start(f32[4,24,144]{2,1,0:T(8,128)} %combine.1), calls=%async_computation.3 | async-start | bytes 196608 | tf_op jit(solution)/shard_map/all_to_all | solution.py:384
  84.9 4.0 %feedback.2.rest_0_ = bf16[144,5120]{1,0:T(8,128)(2,1)} custom-call(s32[3]{0:T(128)S(1)} %pad_add_fusion.place, bf16[4,288,640]{2,1,0:T(8,128)(2,1)} %get-tuple-element.23.total, bf16[4,288,640]{2,1,0:T(8,128)(2,1)} %collective-permute-done.4.total_other, f32[144,256]{1,0:T(8,128)S(1)} %get-tuple-element.25.sums, ...), custom_call_target="tpu_custom_call" | custom-call | flops 1000000000 | bytes 4000000 | tf_op jit(solution)/shard_map/feedback/pallas_call | solution.py:250
  88.9 9.4 %all-to-all-done.3.both = f32[4,24,144]{2,1,0:T(8,128)S(1)} async-done(((f32[4,24,144]{2,1,0:T(8,128)}), f32[4,24,144]{2,1,0:T(8,128)S(1)}, u32[]{:S(2)}, u32[]{:S(2)}) %all-to-all-start.3) | async-done | bytes 55328 | tf_op jit(solution)/shard_map/all_to_all | solution.py:384
  98.3 1.2 %update.1 = (bf16[16,16,144]{2,1,0:T(8,128)(2,1)}, f32[4,144]{1,0:T(4,128)}, f32[4,144]{1,0:T(4,128)}) custom-call(s32[3]{0:T(128)S(1)} %pad_add_fusion.place, f32[4,24,144]{2,1,0:T(8,128)S(1)} %all-to-all-done.3.both), custom_call_target="tpu_custom_call" | custom-call | flops 1000000000 | bytes 4000000 | tf_op jit(solution)/shard_map/update/pallas_call | solution.py:354
  99.6 6.0 %all-to-all-start.4 = ((bf16[16,16,144]{2,1,0:T(8,128)(2,1)}), bf16[16,16,144]{2,1,0:T(8,128)(2,1)S(1)}, u32[]{:S(2)}, u32[]{:S(2)}) async-start(bf16[16,16,144]{2,1,0:T(8,128)(2,1)} %get-tuple-element.28), calls=%async_computation.4 | async-start | bytes 262144 | tf_op jit(solution)/shard_map/all_to_all | solution.py:390
  105.5 4.0 %feedback.3 = bf16[144,5120]{1,0:T(8,128)(2,1)} custom-call(s32[3]{0:T(128)S(1)} %pad_add_fusion.place, bf16[4,288,640]{2,1,0:T(8,128)(2,1)} %get-tuple-element.23.total, bf16[4,288,640]{2,1,0:T(8,128)(2,1)} %collective-permute-done.4.total_other, f32[144,256]{1,0:T(8,128)S(1)} %get-tuple-element.25.sums, ...), custom_call_target="tpu_custom_call", output_to_operand_aliasing={{}: (7, {})} | custom-call | flops 1000000000 | bytes 4000000 | tf_op jit(solution)/shard_map/feedback/pallas_call | solution.py:250
  109.6 2.4 %all-to-all-done.4.updates = bf16[16,16,144]{2,1,0:T(8,128)(2,1)S(1)} async-done(((bf16[16,16,144]{2,1,0:T(8,128)(2,1)}), bf16[16,16,144]{2,1,0:T(8,128)(2,1)S(1)}, u32[]{:S(2)}, u32[]{:S(2)}) %all-to-all-start.4) | async-done | bytes 73760 | tf_op jit(solution)/shard_map/all_to_all | solution.py:390
  111.9 3.2 %weight_step.1 = bf16[144,5120]{1,0:T(8,128)(2,1)} custom-call(s32[3]{0:T(128)S(1)} %pad_add_fusion.place, bf16[16,16,144]{2,1,0:T(8,128)(2,1)S(1)} %all-to-all-done.4.updates, bf16[16,4,16,640]{3,2,1,0:T(8,128)(2,1)S(1)} %copy-done.1, bf16[16,4,16,640]{3,2,1,0:T(8,128)(2,1)S(1)} %collective-permute-done.6.other), custom_call_target="tpu_custom_call" | custom-call | flops 1000000000 | bytes 4000000 | tf_op jit(solution)/shard_map/weight_step/pallas_call | solution.py:297
  (29 shorter events, 4.5 us)
Async XLA Ops:
  0.6 0.7 copy-start.6
  1.3 15.9 %copy-start.4 = (bf16[256,640]{1,0:T(8,128)(2,1)S(1)}, bf16[256,640]{1,0:T(8,128)(2,1)}, u32[]{:S(2)}) copy-start(bf16[256,640]{1,0:T(8,128)(2,1)} %first.1) | copy-start | bytes 983044
  2.0 28.8 %all-to-all-start = ((bf16[16,4,640]{2,1,0:T(4,128)(2,1)}), bf16[16,4,640]{2,1,0:T(4,128)(2,1)S(1)}, u32[]{:S(2)}, u32[]{:S(2)}) async-start(bf16[16,4,640]{2,1,0:T(4,128)(2,1)} %repeat.1), calls=%async_computation | async-start | bytes 163840 | tf_op jit(solution)/shard_map/all_to_all | solution.py:370
  17.2 29.1 %collective-permute-start.1 = (bf16[256,640]{1,0:T(8,128)(2,1)S(1)}, bf16[256,640]{1,0:T(8,128)(2,1)S(1)}, u32[]{:S(2)}, u32[]{:S(2)}) collective-permute-start(bf16[256,640]{1,0:T(8,128)(2,1)S(1)} %copy-done.4), channel_id=1, source_target_pairs={{0,6},{2,4},{4,2},{6,0},{1,7},{3,5},{5,3},{7,1},{8,14},{10,12},{12... | collective-permute-start | bytes 983048 | tf_op jit(solution)/shard_map/ppermute | solution.py:36
  22.8 30.1 %collective-permute-start = (bf16[256,640]{1,0:T(8,128)(2,1)S(1)}, bf16[256,640]{1,0:T(8,128)(2,1)}, u32[]{:S(2)}, u32[]{:S(2)}) collective-permute-start(bf16[256,640]{1,0:T(8,128)(2,1)S(1)} %copy-done.4), channel_id=1, source_target_pairs={{0,4},{2,6},{4,0},{6,2},{1,5},{3,7},{5,1},{7,3},{8,12},{10,14},{12... | collective-permute-start | bytes 983048 | tf_op jit(solution)/shard_map/ppermute | solution.py:36
  30.9 1.1 copy-start.3
  32.0 10.4 %copy-start.2 = (bf16[1,144,5120]{2,1,0:T(8,128)(2,1)S(1)}, bf16[1,144,5120]{2,1,0:T(8,128)(2,1)}, u32[]{:S(2)}) copy-start(bf16[1,144,5120]{2,1,0:T(8,128)(2,1)} %param.8) | copy-start | bytes 4423684
  32.0 10.4 %copy-start.5 = (bf16[256,144]{0,1:T(8,128)(2,1)S(1)}, bf16[256,144]{0,1:T(8,128)(2,1)}, u32[]{:S(2)}) copy-start(bf16[256,144]{0,1:T(8,128)(2,1)} %param.6) | copy-start | bytes 221188
  32.0 23.8 %all-to-all-start.1 = ((bf16[16,4,16,640]{3,2,1,0:T(8,128)(2,1)}), bf16[16,4,16,640]{3,2,1,0:T(8,128)(2,1)S(1)}, u32[]{:S(2)}, u32[]{:S(2)}) async-start(bf16[16,4,16,640]{3,2,1,0:T(8,128)(2,1)} %copy-done.3), calls=%async_computation.1 | async-start | bytes 2621440 | tf_op jit(solution)/shard_map/all_to_all | solution.py:372
  39.6 16.1 %collective-permute-start.3 = (bf16[256,640]{1,0:T(8,128)(2,1)S(1)}, bf16[256,640]{1,0:T(8,128)(2,1)}, u32[]{:S(2)}, u32[]{:S(2)}) collective-permute-start(bf16[256,640]{1,0:T(8,128)(2,1)S(1)} %copy-done.4), channel_id=1, source_target_pairs={{0,2},{2,0},{4,6},{6,4},{1,3},{3,1},{5,7},{7,5},{8,10},{10,8},{12,... | collective-permute-start | bytes 983048 | tf_op jit(solution)/shard_map/ppermute | solution.py:36
  44.4 11.3 %collective-permute-start.2 = (bf16[5,144,640]{2,1,0:T(8,128)(2,1)S(1)}, bf16[5,144,640]{2,1,0:T(8,128)(2,1)S(1)}, u32[]{:S(2)}, u32[]{:S(2)}) collective-permute-start(bf16[5,144,640]{2,1,0:T(8,128)(2,1)S(1)} %pick.1), channel_id=1, source_target_pairs={{0,1},{1,0},{2,3},{3,2},{4,5},{5,4},{6,7},{7,6},{8,9},{9,8},{10,11... | collective-permute-start | bytes 2764808 | tf_op jit(solution)/shard_map/ppermute | solution.py:32
  53.0 25.0 %copy-start.7 = (f32[144,4]{0,1:T(4,128)S(1)}, f32[144,4]{0,1:T(4,128)}, u32[]{:S(2)}) copy-start(f32[144,4]{0,1:T(4,128)} %param.10) | copy-start | bytes 6916
  53.0 25.0 %copy-start.8 = (f32[144,4]{0,1:T(4,128)S(1)}, f32[144,4]{0,1:T(4,128)}, u32[]{:S(2)}) copy-start(f32[144,4]{0,1:T(4,128)} %param.11) | copy-start | bytes 6916
  55.8 1.1 copy-start
  62.5 15.5 %all-to-all-start.2 = ((bf16[32,16,144]{2,1,0:T(8,128)(2,1)}), bf16[32,16,144]{2,1,0:T(8,128)(2,1)S(1)}, u32[]{:S(2)}, u32[]{:S(2)}) async-start(bf16[32,16,144]{2,1,0:T(8,128)(2,1)} %bitcast.7), calls=%async_computation.2 | async-start | bytes 524288 | tf_op jit(solution)/shard_map/all_to_all | solution.py:381
  69.8 15.0 %collective-permute-start.6 = (bf16[16,4,16,640]{3,2,1,0:T(8,128)(2,1)}, bf16[16,4,16,640]{3,2,1,0:T(8,128)(2,1)S(1)}, u32[]{:S(2)}, u32[]{:S(2)}) collective-permute-start(bf16[16,4,16,640]{3,2,1,0:T(8,128)(2,1)} %copy-done), channel_id=1, source_target_pairs={{0,1},{1,0},{2,3},{3,2},{4,5},{5,4},{6,7},{7,6},{8,9},{9,8},{10,11... | collective-permute-start | bytes 3932168 | tf_op jit(solution)/shard_map/ppermute | solution.py:32
  71.9 13.0 %collective-permute-start.5 = (f32[144,256]{1,0:T(8,128)}, f32[144,256]{1,0:T(8,128)S(1)}, u32[]{:S(2)}, u32[]{:S(2)}) collective-permute-start(f32[144,256]{1,0:T(8,128)} %get-tuple-element.26), channel_id=1, source_target_pairs={{0,1},{1,0},{2,3},{3,2},{4,5},{5,4},{6,7},{7,6},{8,9},{9,8},{10,11... | collective-permute-start | bytes 442376 | tf_op jit(solution)/shard_map/ppermute | solution.py:32
  74.1 10.7 %collective-permute-start.4 = (bf16[4,288,640]{2,1,0:T(8,128)(2,1)}, bf16[4,288,640]{2,1,0:T(8,128)(2,1)}, u32[]{:S(2)}, u32[]{:S(2)}) collective-permute-start(bf16[4,288,640]{2,1,0:T(8,128)(2,1)} %get-tuple-element.24), channel_id=1, source_target_pairs={{0,1},{1,0},{2,3},{3,2},{4,5},{5,4},{6,7},{7,6},{8,9},{9,8},{10,11... | collective-permute-start | bytes 4423688 | tf_op jit(solution)/shard_map/ppermute | solution.py:32
  77.9 6.9 %copy-start.1 = (bf16[16,4,16,640]{3,2,1,0:T(8,128)(2,1)S(1)}, bf16[16,4,16,640]{3,2,1,0:T(8,128)(2,1)}, u32[]{:S(2)}) copy-start(bf16[16,4,16,640]{3,2,1,0:T(8,128)(2,1)} %copy-done) | copy-start | bytes 3932164
  78.6 19.7 %all-to-all-start.3 = ((f32[4,24,144]{2,1,0:T(8,128)}), f32[4,24,144]{2,1,0:T(8,128)S(1)}, u32[]{:S(2)}, u32[]{:S(2)}) async-start(f32[4,24,144]{2,1,0:T(8,128)} %combine.1), calls=%async_computation.3 | async-start | bytes 196608 | tf_op jit(solution)/shard_map/all_to_all | solution.py:384
  99.6 12.4 %all-to-all-start.4 = ((bf16[16,16,144]{2,1,0:T(8,128)(2,1)}), bf16[16,16,144]{2,1,0:T(8,128)(2,1)S(1)}, u32[]{:S(2)}, u32[]{:S(2)}) async-start(bf16[16,16,144]{2,1,0:T(8,128)(2,1)} %get-tuple-element.28), calls=%async_computation.4 | async-start | bytes 262144 | tf_op jit(solution)/shard_map/all_to_all | solution.py:390

commit v4 on v3

--- a/solution.py
+++ b/solution.py
@@ -24,7 +24,7 @@
 LONG_COMBINE = 17_000_000_000
 LONG_UPDATE = 1_000_000_000
 LONG_FEEDBACK = 1_000_000_000
-LONG_GRADIENTS = 10_300_000_000
+LONG_GRADIENTS = 12_000_000_000
 f32, bf16 = jnp.float32, jnp.bfloat16
 
 

time: 116 us -> 118 us (1.017)
  the two profiles are of different devices: /device:TPU:2 before, /device:TPU:32 now
where the time goes in v4:
time: 118 us; the launch traced here: 117 us
  starting transfers between devices  57.6 us (49%)
  waiting for transfers between devices  34.4 us (29%)
  Pallas kernels  21.5 us (18%)
  local copies, waits for them, and re-layouts  2.82 us (2%)
    all_to_all x1, starting transfers between devices, local(): along_z = lax.all_to_all(repeat(subspace.T), ('zh', 'zl'), 0, 0)  15.2 us
    all_to_all x1, waiting for transfers between devices, local(): both = lax.all_to_all(both, 'zh', 0, 0)  10.7 us
    ppermute x3, starting transfers between devices, from_xor(): return lax.ppermute(block, 'zl', [(i, i ^ bits) for i in range(4)])  9.56 us
    ppermute x4, starting transfers between devices, swap_cores(): return lax.ppermute(block, 'c', [(0, 1), (1, 0)])  8.44 us
    all_to_all x1, starting transfers between devices, local(): both = lax.all_to_all(both, 'zh', 0, 0)  8.42 us
    pallas_call x2, Pallas kernels, feedback(): pl.pallas_call(functools.partial(feedback_kernel, blocks), out_shape=jax....  8.06 us
    ppermute x3, waiting for transfers between devices, from_xor(): return lax.ppermute(block, 'zl', [(i, i ^ bits) for i in range(4)])  7.65 us
    all_to_all x1, starting transfers between devices, local(): own = lax.all_to_all(spreading, ('x', 'y'), 0, 0)  7.17 us
  transfers between devices with their start and end apart: 12, of which 7 were waited for; matrix products, arithmetic and copies ran while one was open for 0% of the time, Pallas kernels for 9%

profile of v4, /device:TPU:32, one launch (start us, length us, event | category | flops | bytes accessed | tf_op | source)
XLA Modules:
  0.0 117.3 jit_solution(15105089187144889665)
XLA Ops:
  2.0 15.2 %all-to-all-start = ((bf16[16,4,640]{2,1,0:T(4,128)(2,1)}), bf16[16,4,640]{2,1,0:T(4,128)(2,1)S(1)}, u32[]{:S(2)}, u32[]{:S(2)}) async-start(bf16[16,4,640]{2,1,0:T(4,128)(2,1)} %repeat.1), calls=%async_computation | async-start | bytes 163840 | tf_op jit(solution)/shard_map/all_to_all | solution.py:370
  17.2 3.4 %collective-permute-start.1 = (bf16[256,640]{1,0:T(8,128)(2,1)S(1)}, bf16[256,640]{1,0:T(8,128)(2,1)S(1)}, u32[]{:S(2)}, u32[]{:S(2)}) collective-permute-start(bf16[256,640]{1,0:T(8,128)(2,1)S(1)} %copy-done.4), channel_id=1, source_target_pairs={{0,6},{2,4},{4,2},{6,0},{1,7},{3,5},{5,3},{7,1},{8,14},{10,12},{12... | collective-permute-start | bytes 983048 | tf_op jit(solution)/shard_map/ppermute | solution.py:36
  20.6 2.9 %collective-permute-start = (bf16[256,640]{1,0:T(8,128)(2,1)S(1)}, bf16[256,640]{1,0:T(8,128)(2,1)}, u32[]{:S(2)}, u32[]{:S(2)}) collective-permute-start(bf16[256,640]{1,0:T(8,128)(2,1)S(1)} %copy-done.4), channel_id=1, source_target_pairs={{0,4},{2,6},{4,0},{6,2},{1,5},{3,7},{5,1},{7,3},{8,12},{10,14},{12... | collective-permute-start | bytes 983048 | tf_op jit(solution)/shard_map/ppermute | solution.py:36
  23.5 3.3 %collective-permute-start.3 = (bf16[256,640]{1,0:T(8,128)(2,1)S(1)}, bf16[256,640]{1,0:T(8,128)(2,1)}, u32[]{:S(2)}, u32[]{:S(2)}) collective-permute-start(bf16[256,640]{1,0:T(8,128)(2,1)S(1)} %copy-done.4), channel_id=1, source_target_pairs={{0,2},{2,0},{4,6},{6,4},{1,3},{3,1},{5,7},{7,5},{8,10},{10,8},{12,... | collective-permute-start | bytes 983048 | tf_op jit(solution)/shard_map/ppermute | solution.py:36
  26.8 2.9 %all-to-all-done = bf16[16,4,640]{2,1,0:T(4,128)(2,1)S(1)} async-done(((bf16[16,4,640]{2,1,0:T(4,128)(2,1)}), bf16[16,4,640]{2,1,0:T(4,128)(2,1)S(1)}, u32[]{:S(2)}, u32[]{:S(2)}) %all-to-all-start) | async-done | bytes 81952 | tf_op jit(solution)/shard_map/all_to_all | solution.py:370
  30.9 7.2 %all-to-all-start.1 = ((bf16[16,4,16,640]{3,2,1,0:T(8,128)(2,1)}), bf16[16,4,16,640]{3,2,1,0:T(8,128)(2,1)S(1)}, u32[]{:S(2)}, u32[]{:S(2)}) async-start(bf16[16,4,16,640]{3,2,1,0:T(8,128)(2,1)} %copy-done.3), calls=%async_computation.1 | async-start | bytes 2621440 | tf_op jit(solution)/shard_map/all_to_all | solution.py:372
  38.2 2.0 %pick.1 = bf16[5,144,640]{2,1,0:T(8,128)(2,1)S(1)} custom-call(s32[3]{0:T(128)S(1)} %pad_add_fusion.place, bf16[144,5120]{1,0:T(8,128)(2,1)S(1)} %bitcast.14, bf16[144,256]{1,0:T(8,128)(2,1)S(1)} %bitcast.16), custom_call_target="tpu_custom_call" | custom-call | flops 1000000000 | bytes 4000000 | tf_op jit(solution)/shard_map/pick/pallas_call | solution.py:109
  40.1 1.9 %collective-permute-start.2 = (bf16[5,144,640]{2,1,0:T(8,128)(2,1)S(1)}, bf16[5,144,640]{2,1,0:T(8,128)(2,1)S(1)}, u32[]{:S(2)}, u32[]{:S(2)}) collective-permute-start(bf16[5,144,640]{2,1,0:T(8,128)(2,1)S(1)} %pick.1), channel_id=1, source_target_pairs={{0,1},{1,0},{2,3},{3,2},{4,5},{5,4},{6,7},{7,6},{8,9},{9,8},{10,11... | collective-permute-start | bytes 2764808 | tf_op jit(solution)/shard_map/ppermute | solution.py:32
  42.1 2.9 %collective-permute-done.1.second.fourth = bf16[256,640]{1,0:T(8,128)(2,1)S(1)} collective-permute-done((bf16[256,640]{1,0:T(8,128)(2,1)S(1)}, bf16[256,640]{1,0:T(8,128)(2,1)S(1)}, u32[]{:S(2)}, u32[]{:S(2)}) %collective-permute-start.1) | collective-permute-done | bytes 327712 | tf_op jit(solution)/shard_map/ppermute | solution.py:36
  44.9 4.8 %collective-permute-done.first.third = bf16[256,640]{1,0:T(8,128)(2,1)} collective-permute-done((bf16[256,640]{1,0:T(8,128)(2,1)S(1)}, bf16[256,640]{1,0:T(8,128)(2,1)}, u32[]{:S(2)}, u32[]{:S(2)}) %collective-permute-start) | collective-permute-done | bytes 327712 | tf_op jit(solution)/shard_map/ppermute | solution.py:36
  49.7 6.6 %all-to-all-done.1.own = bf16[16,4,16,640]{3,2,1,0:T(8,128)(2,1)S(1)} async-done(((bf16[16,4,16,640]{3,2,1,0:T(8,128)(2,1)}), bf16[16,4,16,640]{3,2,1,0:T(8,128)(2,1)S(1)}, u32[]{:S(2)}, u32[]{:S(2)}) %all-to-all-start.1) | async-done | bytes 1310752 | tf_op jit(solution)/shard_map/all_to_all | solution.py:372
  57.5 5.6 %project.1 = (bf16[2,256,144]{2,1,0:T(8,128)(2,1)}, f32[144,256]{1,0:T(8,128)S(1)}, f32[144,256]{1,0:T(8,128)}, bf16[4,288,640]{2,1,0:T(8,128)(2,1)}, bf16[4,288,640]{2,1,0:T(8,128)(2,1)}) custom-call(s32[3]{0:T(128)S(1)} %pad_add_fusion.place, bf16[144,256]{1,0:T(8,128)(2,1)S(1)} %bitcast.17, bf16[5,144,640]{2,1,0:T(8,128)(2,1)S(1)} %collective-permute-done.2.picked, ...), custom_call_target="tpu_custom_call" | custom-call | flops 1000000000 | bytes 4000000 | tf_op jit(solution)/shard_map/project/pallas_call | solution.py:183
  63.1 4.1 %all-to-all-start.2 = ((bf16[32,16,144]{2,1,0:T(8,128)(2,1)}), bf16[32,16,144]{2,1,0:T(8,128)(2,1)S(1)}, u32[]{:S(2)}, u32[]{:S(2)}) async-start(bf16[32,16,144]{2,1,0:T(8,128)(2,1)} %bitcast.7), calls=%async_computation.2 | async-start | bytes 524288 | tf_op jit(solution)/shard_map/all_to_all | solution.py:381
  67.2 2.2 %collective-permute-start.6 = (bf16[16,4,16,640]{3,2,1,0:T(8,128)(2,1)}, bf16[16,4,16,640]{3,2,1,0:T(8,128)(2,1)S(1)}, u32[]{:S(2)}, u32[]{:S(2)}) collective-permute-start(bf16[16,4,16,640]{3,2,1,0:T(8,128)(2,1)} %copy-done), channel_id=1, source_target_pairs={{0,1},{1,0},{2,3},{3,2},{4,5},{5,4},{6,7},{7,6},{8,9},{9,8},{10,11... | collective-permute-start | bytes 3932168 | tf_op jit(solution)/shard_map/ppermute | solution.py:32
  69.4 2.1 %collective-permute-start.5 = (f32[144,256]{1,0:T(8,128)}, f32[144,256]{1,0:T(8,128)S(1)}, u32[]{:S(2)}, u32[]{:S(2)}) collective-permute-start(f32[144,256]{1,0:T(8,128)} %get-tuple-element.26), channel_id=1, source_target_pairs={{0,1},{1,0},{2,3},{3,2},{4,5},{5,4},{6,7},{7,6},{8,9},{9,8},{10,11... | collective-permute-start | bytes 442376 | tf_op jit(solution)/shard_map/ppermute | solution.py:32
  71.5 2.2 %collective-permute-start.4 = (bf16[4,288,640]{2,1,0:T(8,128)(2,1)}, bf16[4,288,640]{2,1,0:T(8,128)(2,1)}, u32[]{:S(2)}, u32[]{:S(2)}) collective-permute-start(bf16[4,288,640]{2,1,0:T(8,128)(2,1)} %get-tuple-element.24), channel_id=1, source_target_pairs={{0,1},{1,0},{2,3},{3,2},{4,5},{5,4},{6,7},{7,6},{8,9},{9,8},{10,11... | collective-permute-start | bytes 4423688 | tf_op jit(solution)/shard_map/ppermute | solution.py:32
  73.7 2.7 %all-to-all-done.2.part = bf16[32,16,144]{2,1,0:T(8,128)(2,1)S(1)} async-done(((bf16[32,16,144]{2,1,0:T(8,128)(2,1)}), bf16[32,16,144]{2,1,0:T(8,128)(2,1)S(1)}, u32[]{:S(2)}, u32[]{:S(2)}) %all-to-all-start.2) | async-done | bytes 147488 | tf_op jit(solution)/shard_map/all_to_all | solution.py:381
  77.1 8.4 %all-to-all-start.3 = ((f32[4,24,144]{2,1,0:T(8,128)}), f32[4,24,144]{2,1,0:T(8,128)S(1)}, u32[]{:S(2)}, u32[]{:S(2)}) async-start(f32[4,24,144]{2,1,0:T(8,128)} %combine.1), calls=%async_computation.3 | async-start | bytes 196608 | tf_op jit(solution)/shard_map/all_to_all | solution.py:384
  85.6 4.0 %feedback.2.rest_0_ = bf16[144,5120]{1,0:T(8,128)(2,1)} custom-call(s32[3]{0:T(128)S(1)} %pad_add_fusion.place, bf16[4,288,640]{2,1,0:T(8,128)(2,1)} %get-tuple-element.23.total, bf16[4,288,640]{2,1,0:T(8,128)(2,1)} %collective-permute-done.4.total_other, f32[144,256]{1,0:T(8,128)S(1)} %get-tuple-element.25.sums, ...), custom_call_target="tpu_custom_call" | custom-call | flops 1000000000 | bytes 4000000 | tf_op jit(solution)/shard_map/feedback/pallas_call | solution.py:250
  89.6 10.7 %all-to-all-done.3.both = f32[4,24,144]{2,1,0:T(8,128)S(1)} async-done(((f32[4,24,144]{2,1,0:T(8,128)}), f32[4,24,144]{2,1,0:T(8,128)S(1)}, u32[]{:S(2)}, u32[]{:S(2)}) %all-to-all-start.3) | async-done | bytes 55328 | tf_op jit(solution)/shard_map/all_to_all | solution.py:384
  101.5 4.8 %all-to-all-start.4 = ((bf16[16,16,144]{2,1,0:T(8,128)(2,1)}), bf16[16,16,144]{2,1,0:T(8,128)(2,1)S(1)}, u32[]{:S(2)}, u32[]{:S(2)}) async-start(bf16[16,16,144]{2,1,0:T(8,128)(2,1)} %get-tuple-element.28), calls=%async_computation.4 | async-start | bytes 262144 | tf_op jit(solution)/shard_map/all_to_all | solution.py:390
  106.3 4.0 %feedback.3 = bf16[144,5120]{1,0:T(8,128)(2,1)} custom-call(s32[3]{0:T(128)S(1)} %pad_add_fusion.place, bf16[4,288,640]{2,1,0:T(8,128)(2,1)} %get-tuple-element.23.total, bf16[4,288,640]{2,1,0:T(8,128)(2,1)} %collective-permute-done.4.total_other, f32[144,256]{1,0:T(8,128)S(1)} %get-tuple-element.25.sums, ...), custom_call_target="tpu_custom_call", output_to_operand_aliasing={{}: (7, {})} | custom-call | flops 1000000000 | bytes 4000000 | tf_op jit(solution)/shard_map/feedback/pallas_call | solution.py:250
  110.3 3.8 %all-to-all-done.4.updates = bf16[16,16,144]{2,1,0:T(8,128)(2,1)S(1)} async-done(((bf16[16,16,144]{2,1,0:T(8,128)(2,1)}), bf16[16,16,144]{2,1,0:T(8,128)(2,1)S(1)}, u32[]{:S(2)}, u32[]{:S(2)}) %all-to-all-start.4) | async-done | bytes 73760 | tf_op jit(solution)/shard_map/all_to_all | solution.py:390
  114.1 3.2 %weight_step.1 = bf16[144,5120]{1,0:T(8,128)(2,1)} custom-call(s32[3]{0:T(128)S(1)} %pad_add_fusion.place, bf16[16,16,144]{2,1,0:T(8,128)(2,1)S(1)} %all-to-all-done.4.updates, bf16[16,4,16,640]{3,2,1,0:T(8,128)(2,1)S(1)} %copy-done.1, bf16[16,4,16,640]{3,2,1,0:T(8,128)(2,1)S(1)} %collective-permute-done.6.other), custom_call_target="tpu_custom_call" | custom-call | flops 1000000000 | bytes 4000000 | tf_op jit(solution)/shard_map/weight_step/pallas_call | solution.py:297
  (29 shorter events, 5.6 us)
Async XLA Ops:
  0.6 0.7 copy-start.6
  1.3 15.9 %copy-start.4 = (bf16[256,640]{1,0:T(8,128)(2,1)S(1)}, bf16[256,640]{1,0:T(8,128)(2,1)}, u32[]{:S(2)}) copy-start(bf16[256,640]{1,0:T(8,128)(2,1)} %first.1) | copy-start | bytes 983044
  2.0 27.7 %all-to-all-start = ((bf16[16,4,640]{2,1,0:T(4,128)(2,1)}), bf16[16,4,640]{2,1,0:T(4,128)(2,1)S(1)}, u32[]{:S(2)}, u32[]{:S(2)}) async-start(bf16[16,4,640]{2,1,0:T(4,128)(2,1)} %repeat.1), calls=%async_computation | async-start | bytes 163840 | tf_op jit(solution)/shard_map/all_to_all | solution.py:370
  17.2 27.7 %collective-permute-start.1 = (bf16[256,640]{1,0:T(8,128)(2,1)S(1)}, bf16[256,640]{1,0:T(8,128)(2,1)S(1)}, u32[]{:S(2)}, u32[]{:S(2)}) collective-permute-start(bf16[256,640]{1,0:T(8,128)(2,1)S(1)} %copy-done.4), channel_id=1, source_target_pairs={{0,6},{2,4},{4,2},{6,0},{1,7},{3,5},{5,3},{7,1},{8,14},{10,12},{12... | collective-permute-start | bytes 983048 | tf_op jit(solution)/shard_map/ppermute | solution.py:36
  20.6 29.2 %collective-permute-start = (bf16[256,640]{1,0:T(8,128)(2,1)S(1)}, bf16[256,640]{1,0:T(8,128)(2,1)}, u32[]{:S(2)}, u32[]{:S(2)}) collective-permute-start(bf16[256,640]{1,0:T(8,128)(2,1)S(1)} %copy-done.4), channel_id=1, source_target_pairs={{0,4},{2,6},{4,0},{6,2},{1,5},{3,7},{5,1},{7,3},{8,12},{10,14},{12... | collective-permute-start | bytes 983048 | tf_op jit(solution)/shard_map/ppermute | solution.py:36
  23.5 26.2 %collective-permute-start.3 = (bf16[256,640]{1,0:T(8,128)(2,1)S(1)}, bf16[256,640]{1,0:T(8,128)(2,1)}, u32[]{:S(2)}, u32[]{:S(2)}) collective-permute-start(bf16[256,640]{1,0:T(8,128)(2,1)S(1)} %copy-done.4), channel_id=1, source_target_pairs={{0,2},{2,0},{4,6},{6,4},{1,3},{3,1},{5,7},{7,5},{8,10},{10,8},{12,... | collective-permute-start | bytes 983048 | tf_op jit(solution)/shard_map/ppermute | solution.py:36
  29.8 1.1 copy-start.3
  30.9 7.3 %copy-start.2 = (bf16[1,144,5120]{2,1,0:T(8,128)(2,1)S(1)}, bf16[1,144,5120]{2,1,0:T(8,128)(2,1)}, u32[]{:S(2)}) copy-start(bf16[1,144,5120]{2,1,0:T(8,128)(2,1)} %param.8) | copy-start | bytes 4423684
  30.9 7.3 %copy-start.5 = (bf16[256,144]{0,1:T(8,128)(2,1)S(1)}, bf16[256,144]{0,1:T(8,128)(2,1)}, u32[]{:S(2)}) copy-start(bf16[256,144]{0,1:T(8,128)(2,1)} %param.6) | copy-start | bytes 221188
  30.9 25.5 %all-to-all-start.1 = ((bf16[16,4,16,640]{3,2,1,0:T(8,128)(2,1)}), bf16[16,4,16,640]{3,2,1,0:T(8,128)(2,1)S(1)}, u32[]{:S(2)}, u32[]{:S(2)}) async-start(bf16[16,4,16,640]{3,2,1,0:T(8,128)(2,1)} %copy-done.3), calls=%async_computation.1 | async-start | bytes 2621440 | tf_op jit(solution)/shard_map/all_to_all | solution.py:372
  40.1 9.6 %collective-permute-start.2 = (bf16[5,144,640]{2,1,0:T(8,128)(2,1)S(1)}, bf16[5,144,640]{2,1,0:T(8,128)(2,1)S(1)}, u32[]{:S(2)}, u32[]{:S(2)}) collective-permute-start(bf16[5,144,640]{2,1,0:T(8,128)(2,1)S(1)} %pick.1), channel_id=1, source_target_pairs={{0,1},{1,0},{2,3},{3,2},{4,5},{5,4},{6,7},{7,6},{8,9},{9,8},{10,11... | collective-permute-start | bytes 2764808 | tf_op jit(solution)/shard_map/ppermute | solution.py:32
  49.7 26.7 %copy-start.7 = (f32[144,4]{0,1:T(4,128)S(1)}, f32[144,4]{0,1:T(4,128)}, u32[]{:S(2)}) copy-start(f32[144,4]{0,1:T(4,128)} %param.10) | copy-start | bytes 6916
  49.7 26.7 %copy-start.8 = (f32[144,4]{0,1:T(4,128)S(1)}, f32[144,4]{0,1:T(4,128)}, u32[]{:S(2)}) copy-start(f32[144,4]{0,1:T(4,128)} %param.11) | copy-start | bytes 6916
  56.4 1.1 copy-start
  63.1 13.4 %all-to-all-start.2 = ((bf16[32,16,144]{2,1,0:T(8,128)(2,1)}), bf16[32,16,144]{2,1,0:T(8,128)(2,1)S(1)}, u32[]{:S(2)}, u32[]{:S(2)}) async-start(bf16[32,16,144]{2,1,0:T(8,128)(2,1)} %bitcast.7), calls=%async_computation.2 | async-start | bytes 524288 | tf_op jit(solution)/shard_map/all_to_all | solution.py:381
  67.2 18.4 %collective-permute-start.6 = (bf16[16,4,16,640]{3,2,1,0:T(8,128)(2,1)}, bf16[16,4,16,640]{3,2,1,0:T(8,128)(2,1)S(1)}, u32[]{:S(2)}, u32[]{:S(2)}) collective-permute-start(bf16[16,4,16,640]{3,2,1,0:T(8,128)(2,1)} %copy-done), channel_id=1, source_target_pairs={{0,1},{1,0},{2,3},{3,2},{4,5},{5,4},{6,7},{7,6},{8,9},{9,8},{10,11... | collective-permute-start | bytes 3932168 | tf_op jit(solution)/shard_map/ppermute | solution.py:32
  69.4 16.2 %collective-permute-start.5 = (f32[144,256]{1,0:T(8,128)}, f32[144,256]{1,0:T(8,128)S(1)}, u32[]{:S(2)}, u32[]{:S(2)}) collective-permute-start(f32[144,256]{1,0:T(8,128)} %get-tuple-element.26), channel_id=1, source_target_pairs={{0,1},{1,0},{2,3},{3,2},{4,5},{5,4},{6,7},{7,6},{8,9},{9,8},{10,11... | collective-permute-start | bytes 442376 | tf_op jit(solution)/shard_map/ppermute | solution.py:32
  71.5 14.0 %collective-permute-start.4 = (bf16[4,288,640]{2,1,0:T(8,128)(2,1)}, bf16[4,288,640]{2,1,0:T(8,128)(2,1)}, u32[]{:S(2)}, u32[]{:S(2)}) collective-permute-start(bf16[4,288,640]{2,1,0:T(8,128)(2,1)} %get-tuple-element.24), channel_id=1, source_target_pairs={{0,1},{1,0},{2,3},{3,2},{4,5},{5,4},{6,7},{7,6},{8,9},{9,8},{10,11... | collective-permute-start | bytes 4423688 | tf_op jit(solution)/shard_map/ppermute | solution.py:32
  76.4 9.1 %copy-start.1 = (bf16[16,4,16,640]{3,2,1,0:T(8,128)(2,1)S(1)}, bf16[16,4,16,640]{3,2,1,0:T(8,128)(2,1)}, u32[]{:S(2)}) copy-start(bf16[16,4,16,640]{3,2,1,0:T(8,128)(2,1)} %copy-done) | copy-start | bytes 3932164
  77.1 23.1 %all-to-all-start.3 = ((f32[4,24,144]{2,1,0:T(8,128)}), f32[4,24,144]{2,1,0:T(8,128)S(1)}, u32[]{:S(2)}, u32[]{:S(2)}) async-start(f32[4,24,144]{2,1,0:T(8,128)} %combine.1), calls=%async_computation.3 | async-start | bytes 196608 | tf_op jit(solution)/shard_map/all_to_all | solution.py:384
  101.5 12.6 %all-to-all-start.4 = ((bf16[16,16,144]{2,1,0:T(8,128)(2,1)}), bf16[16,16,144]{2,1,0:T(8,128)(2,1)S(1)}, u32[]{:S(2)}, u32[]{:S(2)}) async-start(bf16[16,16,144]{2,1,0:T(8,128)(2,1)} %get-tuple-element.28), calls=%async_computation.4 | async-start | bytes 262144 | tf_op jit(solution)/shard_map/all_to_all | solution.py:390
